TPU v7x, 32 devices: a whole 2x2x4 slice. The times are simulated.
32 devices in a mesh: dp: 16 (over z, y, x), tensor: 2 (over core).
Axes of the slice: x: 2, y: 2, z: 4, core: 2. Of those that a mesh axis runs over, the one named last changes fastest.
Arguments:
- patches: bfloat16 [16, 256, 16], P('dp'), may hold values from -6 to 6
- timesteps: int32 [16], P('dp'), may hold values from 0 to 999
- labels: int32 [16], P('dp'), may hold values from 0 to 1000
- target: float32 [16, 256, 32], P('dp'), may hold values from -6 to 6
- attend_in: float32 [1, 1024, 3072], P(None, 'dp', 'tensor'), may hold values from -0.1875 to 0.1875
- attend_out: float32 [1, 1024, 1024], P(None, 'dp', 'tensor'), may hold values from -0.75 to 0.75
- hidden_in: float32 [1, 1024, 4096], P(None, 'dp', 'tensor'), may hold values from -0.1875 to 0.1875
- hidden_out: float32 [1, 1024, 4096], P(None, 'dp', 'tensor'), may hold values from -0.09375 to 0.09375
- modulation: float32 [8192, 1024], P('dp'), may hold values from -0.1875 to 0.1875
- embedding: float32 [2329, 1024], P(None, 'dp'), may hold values from -6 to 6
- moment_attend_in: float32 [1, 1024, 3072], P(None, 'dp', 'tensor'), may hold values from -0.001953125 to 0.001953125
- moment_attend_out: float32 [1, 1024, 1024], P(None, 'dp', 'tensor'), may hold values from -0.001953125 to 0.001953125
- moment_hidden_in: float32 [1, 1024, 4096], P(None, 'dp', 'tensor'), may hold values from -0.001953125 to 0.001953125
- moment_hidden_out: float32 [1, 1024, 4096], P(None, 'dp', 'tensor'), may hold values from -0.001953125 to 0.001953125
- moment_modulation: float32 [8192, 1024], P('dp'), may hold values from -0.001953125 to 0.001953125
- moment_embedding: float32 [2329, 1024], P(None, 'dp'), may hold values from -0.001953125 to 0.001953125
- square_attend_in: float32 [1, 1024, 3072], P(None, 'dp', 'tensor'), may hold values from 4.1811314e-09 to 6.68981e-08
- square_attend_out: float32 [1, 1024, 1024], P(None, 'dp', 'tensor'), may hold values from 4.1811314e-09 to 6.68981e-08
- square_hidden_in: float32 [1, 1024, 4096], P(None, 'dp', 'tensor'), may hold values from 4.1811314e-09 to 6.68981e-08
- square_hidden_out: float32 [1, 1024, 4096], P(None, 'dp', 'tensor'), may hold values from 4.1811314e-09 to 6.68981e-08
- square_modulation: float32 [8192, 1024], P('dp'), may hold values from 4.1811314e-09 to 6.68981e-08
- square_embedding: float32 [2329, 1024], P(None, 'dp'), may hold values from 4.1811314e-09 to 6.68981e-08
Outputs:
- loss: float32 [], replicated
- prenorm: float32 [], replicated
- update_attend_in: float32 [1, 1024, 3072], P(None, 'dp', 'tensor')
- update_attend_out: float32 [1, 1024, 1024], P(None, 'dp', 'tensor')
- update_hidden_in: float32 [1, 1024, 4096], P(None, 'dp', 'tensor')
- update_hidden_out: float32 [1, 1024, 4096], P(None, 'dp', 'tensor')
- update_modulation: float32 [8192, 1024], P('dp')
- update_embedding: float32 [2329, 1024], P(None, 'dp')
- new_moment_attend_in: float32 [1, 1024, 3072], P(None, 'dp', 'tensor')
- new_moment_attend_out: float32 [1, 1024, 1024], P(None, 'dp', 'tensor')
- new_moment_hidden_in: float32 [1, 1024, 4096], P(None, 'dp', 'tensor')
- new_moment_hidden_out: float32 [1, 1024, 4096], P(None, 'dp', 'tensor')
- new_moment_modulation: float32 [8192, 1024], P('dp')
- new_moment_embedding: float32 [2329, 1024], P(None, 'dp')
- new_square_attend_in: float32 [1, 1024, 3072], P(None, 'dp', 'tensor')
- new_square_attend_out: float32 [1, 1024, 1024], P(None, 'dp', 'tensor')
- new_square_hidden_in: float32 [1, 1024, 4096], P(None, 'dp', 'tensor')
- new_square_hidden_out: float32 [1, 1024, 4096], P(None, 'dp', 'tensor')
- new_square_modulation: float32 [8192, 1024], P('dp')
- new_square_embedding: float32 [2329, 1024], P(None, 'dp')
Inputs may be any that keep to these rules, and one draw needn't show every extreme that they name: `labels`: the label 1001 - 1 is the unconditional class.
All inputs are finite; a program needn't handle non-finite values.
Results may differ from a plain program's by a relative error of at most 0.012.
The roundings to bfloat16 on the way count: a program that leaves them out, or rounds other values in their place, can miss the bound.
Values may be sent and summed in bfloat16 or wider, within the bound.
No kernel may reach another device: no remote copies, remote signals or barrier semaphores. Data moves between devices by JAX's collectives and lax.ppermute only.
A program may use at most 192 MiB of HBM per device.

v0:
```python
from functools import partial
import math

import jax
import jax.numpy as jnp
from jax import lax
from jax.sharding import PartitionSpec as P

D = 1024
HEAD = 64
FREQ = 256
CLASSES = 1001
GRID = 16
LAYERS = 1
STEP = 10
OUT = 32


LN_EPS = 1e-06
BETA_ONE = 0.5
BETA_TWO = 0.5
LEARN_RATE = 0.01
DECAY_RATE = 0.1
ADAM_EPS = 1e-08
CLIP_SCALE = 40.0
NORM_EPS = 1e-06


def times_plain(left_side, right_side):
    return jnp.dot(left_side, right_side, preferred_element_type=jnp.float32)


def times_left_t(left_side, right_side):
    return lax.dot_general(
        left_side, right_side, (((0,), (0,)), ((), ())), preferred_element_type=jnp.float32
    )


def times_right_t(left_side, right_side):
    return lax.dot_general(
        left_side, right_side, (((1,), (1,)), ((), ())), preferred_element_type=jnp.float32
    )


def position_table(feature_count, grid_side):
    quarter = feature_count // 4
    rates = 1.0 / 10000.0 ** (jnp.arange(quarter, dtype=jnp.float32) / quarter)
    cells = jnp.arange(grid_side * grid_side, dtype=jnp.int32)
    column_angle = (cells % grid_side).astype(jnp.float32)[:, None] * rates[None, :]
    row_angle = (cells // grid_side).astype(jnp.float32)[:, None] * rates[None, :]
    return jnp.concatenate(
        [jnp.sin(column_angle), jnp.cos(column_angle), jnp.sin(row_angle), jnp.cos(row_angle)],
        axis=1,
    )


def time_table(step_values, freq_count):
    half_count = freq_count // 2
    rates = jnp.exp(-math.log(10000.0) * jnp.arange(half_count, dtype=jnp.float32) / half_count)
    angles = step_values.astype(jnp.float32)[:, None] * rates[None, :]
    return jnp.concatenate([jnp.cos(angles), jnp.sin(angles)], axis=1)


def modulate(values, shift_vec, scale_vec):
    center = values - jnp.mean(values, axis=-1, keepdims=True)
    normed = center * lax.rsqrt(jnp.mean(center * center, axis=-1, keepdims=True) + LN_EPS)
    return normed * (1.0 + scale_vec) + shift_vec


def modulate_back(values, shift_vec, scale_vec, cotangent):
    _, pullback = jax.vjp(modulate, values, shift_vec, scale_vec)
    return pullback(cotangent)


def silu_back(values, cotangent):
    _, pullback = jax.vjp(jax.nn.silu, values)
    return pullback(cotangent)[0]


def gelu_back(values, cotangent):
    _, pullback = jax.vjp(partial(jax.nn.gelu, approximate=True), values)
    return pullback(cotangent)[0]


def mod_piece(modulators, column_block):
    return modulators[:, None, column_block * D : (column_block + 1) * D]


def score_block(packed):
    return jnp.einsum(
        "bqhe,bkhe->bhqk",
        packed[:, :, :, 0],
        packed[:, :, :, 1],
        preferred_element_type=jnp.float32,
    ) * HEAD ** (-0.5)


def attend_part(stream, shift_vec, scale_vec, weight_qkv):
    images, length = (stream.shape[0], stream.shape[1])
    heads_here = weight_qkv.shape[1] // (3 * HEAD)
    normed = modulate(stream, shift_vec, scale_vec).astype(jnp.bfloat16).reshape(images * length, D)
    packed = (
        times_plain(normed, weight_qkv)
        .astype(jnp.bfloat16)
        .reshape(images, length, heads_here, 3, HEAD)
    )
    scores = score_block(packed)
    row_max = jnp.max(scores, axis=-1, keepdims=True)
    log_total = row_max + jnp.log(jnp.sum(jnp.exp(scores - row_max), axis=-1, keepdims=True))
    attention = jnp.exp(scores - log_total).astype(jnp.bfloat16)
    mixture = jnp.einsum(
        "bhqk,bkhe->bqhe", attention, packed[:, :, :, 2], preferred_element_type=jnp.float32
    )
    return (
        normed,
        packed,
        log_total,
        mixture.astype(jnp.bfloat16).reshape(images * length, heads_here * HEAD),
    )


def attend_grad(packed, log_total, grad_mixture):
    images, length, heads_here = (packed.shape[0], packed.shape[1], packed.shape[2])
    queries, key_rows, values = (packed[:, :, :, 0], packed[:, :, :, 1], packed[:, :, :, 2])
    attention = jnp.exp(score_block(packed) - log_total)
    grad_values = jnp.einsum(
        "bhqk,bqhe->bkhe",
        attention.astype(jnp.bfloat16),
        grad_mixture,
        preferred_element_type=jnp.float32,
    )
    grad_attention = jnp.einsum(
        "bqhe,bkhe->bhqk", grad_mixture, values, preferred_element_type=jnp.float32
    )
    grad_scores = attention * (
        grad_attention - jnp.sum(attention * grad_attention, axis=-1, keepdims=True)
    )
    grad_scores = grad_scores.astype(jnp.bfloat16)
    grad_queries = jnp.einsum(
        "bhqk,bkhe->bqhe", grad_scores, key_rows, preferred_element_type=jnp.float32
    ) * HEAD ** (-0.5)
    grad_keys = jnp.einsum(
        "bhqk,bqhe->bkhe", grad_scores, queries, preferred_element_type=jnp.float32
    ) * HEAD ** (-0.5)
    stacked = jnp.stack([grad_queries, grad_keys, grad_values], axis=3)
    return stacked.astype(jnp.bfloat16).reshape(images * length, heads_here * 3 * HEAD)


def expand_part(stream, shift_vec, scale_vec, weight_inner):
    images, length = (stream.shape[0], stream.shape[1])
    normed = modulate(stream, shift_vec, scale_vec).astype(jnp.bfloat16).reshape(images * length, D)
    inner_pre = times_plain(normed, weight_inner)
    active = jax.nn.gelu(inner_pre, approximate=True).astype(jnp.bfloat16)
    return (normed, inner_pre, active)


def adam_update(master, moment, square, gradient, factor):
    clipped = gradient * factor
    new_moment = BETA_ONE * moment + (1.0 - BETA_ONE) * clipped
    new_square = BETA_TWO * square + (1.0 - BETA_TWO) * clipped * clipped
    first_hat = new_moment / (1.0 - BETA_ONE**STEP)
    second_hat = new_square / (1.0 - BETA_TWO**STEP)
    change = -LEARN_RATE * (first_hat / (jnp.sqrt(second_hat) + ADAM_EPS) + DECAY_RATE * master)
    return (change, new_moment, new_square)


def local(
    patches,
    timesteps,
    labels,
    target,
    attend_in,
    attend_out,
    hidden_in,
    hidden_out,
    modulation,
    embedding,
    moment_attend_in,
    moment_attend_out,
    moment_hidden_in,
    moment_hidden_out,
    moment_modulation,
    moment_embedding,
    square_attend_in,
    square_attend_out,
    square_hidden_in,
    square_hidden_out,
    square_modulation,
    square_embedding,
):
    images, length, patch_width = patches.shape
    tokens_all = images * length * lax.axis_size("dp")
    entries = tokens_all * OUT
    local_modulation = modulation.astype(jnp.bfloat16)
    (
        full_attend_in,
        full_attend_out,
        full_hidden_in,
        full_hidden_out,
        full_modulation,
        full_embedding,
    ) = (
        lax.all_gather(attend_in.astype(jnp.bfloat16), "dp", axis=1, tiled=True),
        lax.all_gather(attend_out.astype(jnp.bfloat16), "dp", axis=1, tiled=True),
        lax.all_gather(hidden_in.astype(jnp.bfloat16), "dp", axis=1, tiled=True),
        lax.all_gather(hidden_out.astype(jnp.bfloat16), "dp", axis=1, tiled=True),
        lax.all_gather(local_modulation, "dp", axis=0, tiled=True),
        lax.all_gather(embedding.astype(jnp.bfloat16), "dp", axis=1, tiled=True),
    )
    rows_two = patch_width + FREQ
    rows_class = rows_two + D
    rows_head = rows_class + CLASSES
    patch_proj = full_embedding[:patch_width]
    time_one = full_embedding[patch_width:rows_two]
    time_two = full_embedding[rows_two:rows_class]
    class_table = full_embedding[rows_class:rows_head]
    head_rows = full_embedding[rows_head:]
    frequencies = time_table(timesteps, FREQ).astype(jnp.bfloat16)
    time_pre = times_plain(frequencies, time_one)
    time_act = jax.nn.silu(time_pre).astype(jnp.bfloat16)
    one_hot = labels[:, None] == jnp.arange(CLASSES, dtype=jnp.int32)[None, :]
    condition = times_plain(time_act, time_two) + times_plain(
        one_hot.astype(jnp.bfloat16), class_table
    )
    cond_act = jax.nn.silu(condition).astype(jnp.bfloat16)
    modulators = times_right_t(cond_act, full_modulation)
    tokens_flat = patches.reshape(images * length, patch_width)
    stream = (
        times_plain(tokens_flat, patch_proj).reshape(images, length, D)
        + position_table(D, GRID)[None]
    )
    layer_index = 0
    offset = 6 * layer_index
    stream_in = stream
    normed_attend, packed, log_total, mixture = attend_part(
        stream_in,
        mod_piece(modulators, offset),
        mod_piece(modulators, offset + 1),
        full_attend_in[layer_index],
    )
    branch_attend = lax.psum(
        times_right_t(mixture, full_attend_out[layer_index]), "tensor"
    ).reshape(images, length, D)
    stream_mid = stream_in + mod_piece(modulators, offset + 2) * branch_attend
    normed_expand, inner_pre, active = expand_part(
        stream_mid,
        mod_piece(modulators, offset + 3),
        mod_piece(modulators, offset + 4),
        full_hidden_in[layer_index],
    )
    branch_expand = (
        lax.psum(times_right_t(active, full_hidden_out[layer_index]).astype(jnp.bfloat16), "tensor")
        .astype(jnp.float32)
        .reshape(images, length, D)
    )
    stream = stream_mid + mod_piece(modulators, offset + 5) * branch_expand
    stored = [(stream_in, stream_mid, branch_attend, branch_expand)]
    shift_final = mod_piece(modulators, 6 * LAYERS)
    scale_final = mod_piece(modulators, 6 * LAYERS + 1)
    final_normed = (
        modulate(stream, shift_final, scale_final).astype(jnp.bfloat16).reshape(images * length, D)
    )
    output = times_right_t(final_normed, head_rows)
    residue = output - target.reshape(images * length, OUT)
    local_loss = jnp.sum(residue * residue)
    grad_output = (residue * (2.0 / entries)).astype(jnp.bfloat16)
    grad_head = times_left_t(grad_output, final_normed)
    grad_final = times_plain(grad_output, head_rows)
    grad_stream, grad_shift_final, grad_scale_final = modulate_back(
        stream, shift_final, scale_final, grad_final.reshape(images, length, D)
    )
    grad_slots = [None] * (6 * LAYERS)
    grad_qkv_list = [None] * LAYERS
    grad_proj_list = [None] * LAYERS
    grad_inner_list = [None] * LAYERS
    grad_outer_list = [None] * LAYERS
    for layer_index in reversed(range(LAYERS)):
        offset = 6 * layer_index
        stream_in, stream_mid, branch_attend, branch_expand = stored[layer_index]
        normed_attend, packed, log_total, mixture = attend_part(
            stream_in,
            mod_piece(modulators, offset),
            mod_piece(modulators, offset + 1),
            full_attend_in[layer_index],
        )
        normed_expand, inner_pre, active = expand_part(
            stream_mid,
            mod_piece(modulators, offset + 3),
            mod_piece(modulators, offset + 4),
            full_hidden_in[layer_index],
        )
        grad_gate_expand = jnp.sum(grad_stream * branch_expand, axis=1, keepdims=True)
        grad_branch = (
            (mod_piece(modulators, offset + 5) * grad_stream)
            .astype(jnp.bfloat16)
            .reshape(images * length, D)
        )
        grad_outer_list[layer_index] = times_left_t(grad_branch, active)
        grad_active = times_plain(grad_branch, full_hidden_out[layer_index])
        grad_inner = gelu_back(inner_pre, grad_active).astype(jnp.bfloat16)
        grad_inner_list[layer_index] = times_left_t(normed_expand, grad_inner)
        grad_normed = lax.psum(
            times_right_t(grad_inner, full_hidden_in[layer_index]).astype(jnp.bfloat16), "tensor"
        ).astype(jnp.float32)
        part_stream, grad_shift_expand, grad_scale_expand = modulate_back(
            stream_mid,
            mod_piece(modulators, offset + 3),
            mod_piece(modulators, offset + 4),
            grad_normed.reshape(images, length, D),
        )
        grad_stream = grad_stream + part_stream
        grad_gate_attend = jnp.sum(grad_stream * branch_attend, axis=1, keepdims=True)
        grad_branch = (
            (mod_piece(modulators, offset + 2) * grad_stream)
            .astype(jnp.bfloat16)
            .reshape(images * length, D)
        )
        grad_proj_list[layer_index] = times_left_t(grad_branch, mixture)
        heads_here = packed.shape[2]
        grad_mixture = (
            times_plain(grad_branch, full_attend_out[layer_index])
            .astype(jnp.bfloat16)
            .reshape(images, length, heads_here, HEAD)
        )
        grad_packed = attend_grad(packed, log_total, grad_mixture)
        grad_qkv_list[layer_index] = times_left_t(normed_attend, grad_packed)
        grad_normed = lax.psum(
            times_right_t(grad_packed, full_attend_in[layer_index]).astype(jnp.bfloat16), "tensor"
        ).astype(jnp.float32)
        part_stream, grad_shift_attend, grad_scale_attend = modulate_back(
            stream_in,
            mod_piece(modulators, offset),
            mod_piece(modulators, offset + 1),
            grad_normed.reshape(images, length, D),
        )
        grad_stream = grad_stream + part_stream
        grad_slots[offset : offset + 6] = [
            grad_shift_attend,
            grad_scale_attend,
            grad_gate_attend,
            grad_shift_expand,
            grad_scale_expand,
            grad_gate_expand,
        ]
    grad_slots = grad_slots + [grad_shift_final, grad_scale_final]
    grad_modulators = jnp.concatenate(
        [grad_item[:, 0, :] for grad_item in grad_slots], axis=1
    ).astype(jnp.bfloat16)
    grad_modulation = times_left_t(grad_modulators, cond_act)
    grad_cond_act = times_plain(grad_modulators, full_modulation)
    grad_condition = silu_back(condition, grad_cond_act)
    grad_class = lax.dot_general(
        one_hot.astype(jnp.float32),
        grad_condition,
        (((0,), (0,)), ((), ())),
        precision=lax.Precision.HIGHEST,
        preferred_element_type=jnp.float32,
    )
    grad_time_embed = grad_condition.astype(jnp.bfloat16)
    grad_time_two = times_left_t(time_act, grad_time_embed)
    grad_time_pre = silu_back(time_pre, times_right_t(grad_time_embed, time_two)).astype(
        jnp.bfloat16
    )
    grad_time_one = times_left_t(frequencies, grad_time_pre)
    grad_patch = times_left_t(
        tokens_flat, grad_stream.astype(jnp.bfloat16).reshape(images * length, D)
    )
    grad_embedding = jnp.concatenate(
        [grad_patch, grad_time_one, grad_time_two, grad_class, grad_head], axis=0
    )
    grad_attend_in = jnp.stack(grad_qkv_list, axis=0)
    grad_attend_out = jnp.stack(grad_proj_list, axis=0)
    grad_hidden_in = jnp.stack(grad_inner_list, axis=0)
    grad_hidden_out = jnp.stack(grad_outer_list, axis=0)
    (
        owned_attend_in,
        owned_attend_out,
        owned_hidden_in,
        owned_hidden_out,
        owned_modulation,
        owned_embedding,
    ) = (
        lax.psum_scatter(grad_attend_in, "dp", scatter_dimension=1, tiled=True),
        lax.psum_scatter(grad_attend_out, "dp", scatter_dimension=1, tiled=True),
        lax.psum_scatter(grad_hidden_in, "dp", scatter_dimension=1, tiled=True),
        lax.psum_scatter(grad_hidden_out, "dp", scatter_dimension=1, tiled=True),
        lax.psum_scatter(grad_modulation, "dp", scatter_dimension=0, tiled=True),
        lax.psum_scatter(grad_embedding, "dp", scatter_dimension=1, tiled=True),
    )
    split_square = (
        jnp.sum(owned_attend_in * owned_attend_in)
        + jnp.sum(owned_attend_out * owned_attend_out)
        + jnp.sum(owned_hidden_in * owned_hidden_in)
        + jnp.sum(owned_hidden_out * owned_hidden_out)
    )
    shared_square = jnp.sum(owned_modulation * owned_modulation) + jnp.sum(
        owned_embedding * owned_embedding
    )
    loss_total, square_total = lax.psum(
        (local_loss * 0.5, split_square + 0.5 * shared_square), ("dp", "tensor")
    )
    loss_value = loss_total / entries
    prenorm = jnp.sqrt(square_total)
    factor = jnp.minimum(1.0, CLIP_SCALE / math.sqrt(tokens_all) / (prenorm + NORM_EPS))
    masters = (attend_in, attend_out, hidden_in, hidden_out, modulation, embedding)
    moments = (
        moment_attend_in,
        moment_attend_out,
        moment_hidden_in,
        moment_hidden_out,
        moment_modulation,
        moment_embedding,
    )
    squares_old = (
        square_attend_in,
        square_attend_out,
        square_hidden_in,
        square_hidden_out,
        square_modulation,
        square_embedding,
    )
    owned = (
        owned_attend_in,
        owned_attend_out,
        owned_hidden_in,
        owned_hidden_out,
        owned_modulation,
        owned_embedding,
    )
    results = [
        adam_update(masters[slot], moments[slot], squares_old[slot], owned[slot], factor)
        for slot in range(6)
    ]
    return (
        loss_value,
        prenorm,
        results[0][0],
        results[1][0],
        results[2][0],
        results[3][0],
        results[4][0],
        results[5][0],
        results[0][1],
        results[1][1],
        results[2][1],
        results[3][1],
        results[4][1],
        results[5][1],
        results[0][2],
        results[1][2],
        results[2][2],
        results[3][2],
        results[4][2],
        results[5][2],
    )


def solution(mesh):
    return jax.shard_map(
        local,
        mesh=mesh,
        in_specs=(
            P("dp", None, None),
            P("dp"),
            P("dp"),
            P("dp", None, None),
            P(None, "dp", "tensor"),
            P(None, "dp", "tensor"),
            P(None, "dp", "tensor"),
            P(None, "dp", "tensor"),
            P("dp", None),
            P(None, "dp"),
            P(None, "dp", "tensor"),
            P(None, "dp", "tensor"),
            P(None, "dp", "tensor"),
            P(None, "dp", "tensor"),
            P("dp", None),
            P(None, "dp"),
            P(None, "dp", "tensor"),
            P(None, "dp", "tensor"),
            P(None, "dp", "tensor"),
            P(None, "dp", "tensor"),
            P("dp", None),
            P(None, "dp"),
        ),
        out_specs=(
            P(),
            P(),
            P(None, "dp", "tensor"),
            P(None, "dp", "tensor"),
            P(None, "dp", "tensor"),
            P(None, "dp", "tensor"),
            P("dp", None),
            P(None, "dp"),
            P(None, "dp", "tensor"),
            P(None, "dp", "tensor"),
            P(None, "dp", "tensor"),
            P(None, "dp", "tensor"),
            P("dp", None),
            P(None, "dp"),
            P(None, "dp", "tensor"),
            P(None, "dp", "tensor"),
            P(None, "dp", "tensor"),
            P(None, "dp", "tensor"),
            P("dp", None),
            P(None, "dp"),
        ),
        check_vma=False,
    )
```

profile of v0, /device:TPU:0, one launch (start us, length us, event | category | flops | bytes accessed | tf_op | source)
XLA Modules:
  0.0 2259.6 jit_solution(4520886412463227390)
XLA Ops:
  7.3 1.8 convert_element_type.171
  9.2 2.8 convert_element_type.177
  15.5 1.9 multiply_sine_fusion.1
  17.4 79.3 %all-gather.7.cloned.1.call-done = bf16[2329,1024]{0,1:T(8,128)(2,1)} async-done(((bf16[2329,64]{0,1:T(8,128)(2,1)}), bf16[2329,1024]{0,1:T(8,128)(2,1)}) %all-gather.7.cloned.1.call-update) | async-done | bytes 4769808 | tf_op jit(solution)/shard_map/all_gather | solution.py:208
  98.8 2.5 fusion.23
  101.4 2.6 fusion.29
  106.2 184.1 %all-gather.9.cloned.1.call-done = bf16[8192,1024]{1,0:T(8,128)(2,1)} async-done(((bf16[512,1024]{1,0:T(8,128)(2,1)}), bf16[8192,1024]{1,0:T(8,128)(2,1)}) %all-gather.9.cloned.1.call-update) | async-done | bytes 16777232 | tf_op jit(solution)/shard_map/all_gather | solution.py:207
  290.4 10.2 fusion.110
  300.6 59.4 %all-gather.11.cloned.1.call-done = bf16[1,1024,1536]{2,1,0:T(8,128)(2,1)} async-done(((bf16[1,64,1536]{2,1,0:T(8,128)(2,1)}), bf16[1,1024,1536]{2,1,0:T(8,128)(2,1)}) %all-gather.11.cloned.1.call-update) | async-done | bytes 3145744 | tf_op jit(solution)/shard_map/all_gather | solution.py:203
  360.1 3.0 fusion.12
  364.7 52.3 %all-gather.13.cloned.1.call-done = bf16[1,1024,512]{2,1,0:T(8,128)(2,1)} async-done(((bf16[1,64,512]{2,1,0:T(8,128)(2,1)}), bf16[1,1024,512]{2,1,0:T(8,128)(2,1)}) %all-gather.13.cloned.1.call-update) | async-done | bytes 1048592 | tf_op jit(solution)/shard_map/all_gather | solution.py:204
  417.1 2.7 fusion.54
  422.7 15.7 all-reduce.6.cloned.1.call-done
  440.4 78.8 %all-gather.15.cloned.1.call-done = bf16[1,1024,2048]{2,1,0:T(8,128)(2,1)} async-done(((bf16[1,64,2048]{2,1,0:T(8,128)(2,1)}), bf16[1,1024,2048]{2,1,0:T(8,128)(2,1)}) %all-gather.15.cloned.1.call-update) | async-done | bytes 4194320 | tf_op jit(solution)/shard_map/all_gather | solution.py:205
  519.3 4.9 fusion.6
  524.1 73.6 %all-gather.17.cloned.1.call-done = bf16[1,1024,2048]{2,1,0:T(8,128)(2,1)} async-done(((bf16[1,64,2048]{2,1,0:T(8,128)(2,1)}), bf16[1,1024,2048]{2,1,0:T(8,128)(2,1)}) %all-gather.17.cloned.1.call-update) | async-done | bytes 4194320 | tf_op jit(solution)/shard_map/all_gather | solution.py:206
  597.7 5.1 fusion.38
  602.9 17.4 all-reduce.8.cloned.1.call-done
  622.1 2.3 multiply_reduce_fusion.14
  624.4 2.3 multiply_reduce_fusion.3
  628.7 2.3 fusion.21
  632.1 2.1 fusion.35
  634.4 19.8 all-reduce.10.cloned.1.call-done
  655.8 2.2 fusion.51
  667.5 1.8 fusion.32
  669.5 2.6 convolution_bitcast_fusion.3
  672.7 4.9 convolution_bitcast_fusion.2
  678.3 6.0 convolution_bitcast_fusion.1
  685.6 6.5 convolution_bitcast_fusion
  697.7 8.2 fusion.111
  706.7 2.5 fusion.27
  709.4 2.3 broadcast_multiply_fusion.2
  711.7 2.4 broadcast_multiply_fusion.1
  714.1 11.6 concatenate.33
  726.4 11.1 broadcast_multiply_fusion
  738.2 35.8 %reduce-scatter.9.cloned.1.call-done = f32[1,64,512]{2,1,0:T(8,128)} async-done(((f32[1,1024,512]{2,1,0:T(8,128)}), f32[1,64,512]{2,1,0:T(8,128)}) %reduce-scatter.9.cloned.1.call-update) | async-done | bytes 131088 | tf_op jit(solution)/shard_map/reduce_scatter | solution.py:384
  775.5 146.5 %reduce-scatter.7.cloned.1.call-done = f32[1,64,1536]{2,1,0:T(8,128)} async-done(((f32[1,1024,1536]{2,1,0:T(8,128)}), f32[1,64,1536]{2,1,0:T(8,128)}) %reduce-scatter.7.cloned.1.call-update) | async-done | bytes 393232 | tf_op jit(solution)/shard_map/reduce_scatter | solution.py:383
  925.0 176.3 %reduce-scatter.11.cloned.1.call-done = f32[1,64,2048]{2,1,0:T(8,128)} async-done(((f32[1,1024,2048]{2,1,0:T(8,128)}), f32[1,64,2048]{2,1,0:T(8,128)}) %reduce-scatter.11.cloned.1.call-update) | async-done | bytes 524304 | tf_op jit(solution)/shard_map/reduce_scatter | solution.py:385
  1101.3 1.8 multiply_reduce_fusion.11
  1103.8 179.9 %reduce-scatter.13.cloned.1.call-done = f32[1,64,2048]{2,1,0:T(8,128)} async-done(((f32[1,1024,2048]{2,1,0:T(8,128)}), f32[1,64,2048]{2,1,0:T(8,128)}) %reduce-scatter.13.cloned.1.call-update) | async-done | bytes 524304 | tf_op jit(solution)/shard_map/reduce_scatter | solution.py:386
  1283.7 1.8 multiply_reduce_fusion.10
  1286.1 211.4 %reduce-scatter.17.cloned.1.call-done = f32[2329,64]{0,1:T(8,128)} async-done(((f32[2329,1024]{0,1:T(8,128)}), f32[2329,64]{0,1:T(8,128)}) %reduce-scatter.17.cloned.1.call-update) | async-done | bytes 596240 | tf_op jit(solution)/shard_map/reduce_scatter | solution.py:388
  1497.5 1.8 multiply_reduce_fusion.9
  1499.4 686.5 %reduce-scatter.15.cloned.1.call-done = f32[512,1024]{1,0:T(8,128)} async-done(((f32[8192,1024]{1,0:T(8,128)}), f32[512,1024]{1,0:T(8,128)}) %reduce-scatter.15.cloned.1.call-update) | async-done | bytes 2097168 | tf_op jit(solution)/shard_map/reduce_scatter | solution.py:387
  2185.9 2.7 multiply_reduce_fusion
  2190.1 44.8 %all-reduce = (f32[]{:T(128)}, f32[]{:T(128)}) all-reduce(f32[]{:T(128)S(6)} %mul.695, f32[]{:T(128)S(6)} %add.350), channel_id=1, replica_groups=mesh['dp'=16,'tensor'=2] {'dp','tensor'}, use_global_device_ids=true, to_apply=%region_11.12 | all-reduce | flops 2 | bytes 16 | tf_op jit(solution)/shard_map/psum | solution.py:399
  2237.1 2.5 add_multiply_fusion.4
  2246.2 4.1 add_multiply_fusion
  (286 shorter events, 49.6 us)
Async XLA Ops:
  7.2 97.4 %copy-start = (bf16[1,256,16]{1,2,0:T(8,128)(2,1)S(1)}, bf16[1,256,16]{1,2,0:T(8,128)(2,1)}, u32[]{:S(2)}) copy-start(bf16[1,256,16]{1,2,0:T(8,128)(2,1)} %param.22) | copy-start | bytes 24580
  7.2 89.6 %all-gather.7.cloned.1.call-start = ((), (), s32[]{:S(2)}) async-start(), calls=%async_computation.6 | async-start | bytes 5292032 | tf_op jit(solution)/shard_map/all_gather | solution.py:208
  9.1 281.2 %all-gather.9.cloned.1.call-start = ((), (), s32[]{:S(2)}) async-start(), calls=%async_computation.7 | async-start | bytes 17825792 | tf_op jit(solution)/shard_map/all_gather | solution.py:207
  12.0 348.1 %all-gather.11.cloned.1.call-start = ((), (), s32[]{:S(2)}) async-start(), calls=%async_computation.8 | async-start | bytes 3342336 | tf_op jit(solution)/shard_map/all_gather | solution.py:203
  12.8 404.3 %all-gather.13.cloned.1.call-start = ((), (), s32[]{:S(2)}) async-start(), calls=%async_computation.9 | async-start | bytes 1114112 | tf_op jit(solution)/shard_map/all_gather | solution.py:204
  13.5 424.9 %all-reduce.6.cloned.1.call-start = ((), (), s32[]{:S(2)}) async-start(), calls=%async_computation.10 | async-start | bytes 2097152 | tf_op jit(solution)/shard_map/psum | solution.py:241
  98.2 5.7 copy-start.63
  105.9 254.1 %copy-start.1 = (f32[256,1024]{1,0:T(8,128)}, f32[256,1024]{1,0:T(8,128)S(1)}, u32[]{:S(2)}) copy-start(f32[256,1024]{1,0:T(8,128)S(1)} %get-tuple-element.81) | copy-start | bytes 3145732
  106.0 254.1 %copy-start.61 = (f32[256]{0:T(256)}, f32[256]{0:T(256)S(1)}, u32[]{:S(2)}) copy-start(f32[256]{0:T(256)S(1)} %broadcast_multiply_fusion.6) | copy-start | bytes 3076
  106.2 184.1 %copy-start.75 = (f32[256]{0:T(256)}, f32[256]{0:T(256)S(1)}, u32[]{:S(2)}) copy-start(f32[256]{0:T(256)S(1)} %multiply_reduce_fusion.8) | copy-start | bytes 3076
  106.2 253.8 %copy-start.70 = (f32[256]{0:T(256)}, f32[256]{0:T(256)S(1)}, u32[]{:S(2)}) copy-start(f32[256]{0:T(256)S(1)} %fusion.84) | copy-start | bytes 3076
  300.6 62.5 %copy-start.56 = (f32[1,1024]{1,0:T(1,128)}, f32[1,1024]{1,0:T(1,128)S(1)}, u32[]{:S(2)}) copy-start(f32[1,1024]{1,0:T(1,128)S(1)} %get-tuple-element.70) | copy-start | bytes 12292
  300.6 218.7 %copy-start.54 = (f32[1,1024]{1,0:T(1,128)}, f32[1,1024]{1,0:T(1,128)S(1)}, u32[]{:S(2)}) copy-start(f32[1,1024]{1,0:T(1,128)S(1)} %get-tuple-element.67) | copy-start | bytes 12292
  300.6 326.6 %copy-start.48 = (f32[1,1024]{1,0:T(1,128)}, f32[1,1024]{1,0:T(1,128)S(1)}, u32[]{:S(2)}) copy-start(f32[1,1024]{1,0:T(1,128)S(1)} %get-tuple-element.69) | copy-start | bytes 12292
  300.6 358.6 %copy-start.58 = (f32[1,1024]{1,0:T(1,128)}, f32[1,1024]{1,0:T(1,128)S(1)}, u32[]{:S(2)}) copy-start(f32[1,1024]{1,0:T(1,128)S(1)} %get-tuple-element.72) | copy-start | bytes 12292
  364.2 55.6 %copy-start.50 = (f32[8,256]{1,0:T(8,128)}, f32[8,256]{1,0:T(8,128)S(1)}, u32[]{:S(2)}) copy-start(f32[8,256]{1,0:T(8,128)S(1)} %log_add_fusion) | copy-start | bytes 24580
  364.7 56.9 %copy-start.22 = (bf16[8,64,256]{2,1,0:T(8,128)(2,1)}, bf16[8,64,256]{2,1,0:T(8,128)(2,1)S(1)}, u32[]{:S(2)}) copy-start(bf16[8,64,256]{2,1,0:T(8,128)(2,1)S(1)} %convolution_convert_fusion.1) | copy-start | bytes 786436
  417.1 4.7 copy-start.26
  419.8 99.4 %all-gather.15.cloned.1.call-start = ((), (), s32[]{:S(2)}) async-start(), calls=%async_computation.11 | async-start | bytes 4456448 | tf_op jit(solution)/shard_map/all_gather | solution.py:205
  421.7 176.0 %all-gather.17.cloned.1.call-start = ((), (), s32[]{:S(2)}) async-start(), calls=%async_computation.12 | async-start | bytes 4456448 | tf_op jit(solution)/shard_map/all_gather | solution.py:206
  422.5 197.8 %all-reduce.8.cloned.1.call-start = ((), (), s32[]{:S(2)}) async-start(), calls=%async_computation.13 | async-start | bytes 1048576 | tf_op jit(solution)/shard_map/psum | solution.py:252
  440.1 217.8 %copy-start.59 = (f32[256]{0:T(256)}, f32[256]{0:T(256)S(1)}, u32[]{:S(2)}) copy-start(f32[256]{0:T(256)S(1)} %broadcast_multiply_fusion.5) | copy-start | bytes 3076
  440.4 217.6 %copy-start.66 = (f32[256]{0:T(256)}, f32[256]{0:T(256)S(1)}, u32[]{:S(2)}) copy-start(f32[256]{0:T(256)S(1)} %fusion.85) | copy-start | bytes 3076
  602.8 51.4 %all-reduce.10.cloned.1.call-start = ((), (), s32[]{:S(2)}) async-start(), calls=%async_computation.14 | async-start | bytes 1048576 | tf_op jit(solution)/shard_map/psum | solution.py:302
  622.1 4.6 copy-start.15
  622.1 6.0 copy-start.84
  627.2 30.8 %copy-start.68 = (f32[256]{0:T(256)}, f32[256]{0:T(256)S(1)}, u32[]{:S(2)}) copy-start(f32[256]{0:T(256)S(1)} %negate_multiply_fusion.2) | copy-start | bytes 3076
  634.2 60.2 %all-reduce.12.cloned.1.call-start = ((), (), s32[]{:S(2)}) async-start(), calls=%async_computation.19 | async-start | bytes 1048576 | tf_op jit(solution)/shard_map/psum | solution.py:327
  669.4 104.6 %reduce-scatter.9.cloned.1.call-start = ((), (), s32[]{:S(2)}) async-start(), calls=%async_computation.16 | async-start | bytes 2228224 | tf_op jit(solution)/shard_map/reduce_scatter | solution.py:384
  672.1 249.9 %reduce-scatter.7.cloned.1.call-start = ((), (), s32[]{:S(2)}) async-start(), calls=%async_computation.15 | async-start | bytes 6684672 | tf_op jit(solution)/shard_map/reduce_scatter | solution.py:383
  677.7 423.6 %reduce-scatter.11.cloned.1.call-start = ((), (), s32[]{:S(2)}) async-start(), calls=%async_computation.17 | async-start | bytes 8912896 | tf_op jit(solution)/shard_map/reduce_scatter | solution.py:385
  684.4 599.3 %reduce-scatter.13.cloned.1.call-start = ((), (), s32[]{:S(2)}) async-start(), calls=%async_computation.18 | async-start | bytes 8912896 | tf_op jit(solution)/shard_map/reduce_scatter | solution.py:386
  692.1 4.9 copy-start.76
  692.1 805.5 %reduce-scatter.17.cloned.1.call-start = ((), (), s32[]{:S(2)}) async-start(), calls=%async_computation.21 | async-start | bytes 10584064 | tf_op jit(solution)/shard_map/reduce_scatter | solution.py:388
  697.7 8.2 copy-start.73
  725.7 1460.2 %reduce-scatter.15.cloned.1.call-start = ((), (), s32[]{:S(2)}) async-start(), calls=%async_computation.20 | async-start | bytes 35651584 | tf_op jit(solution)/shard_map/reduce_scatter | solution.py:387
  775.5 1460.8 %copy-start.41 = (f32[1,64,512]{2,1,0:T(8,128)S(1)}, f32[1,64,512]{2,1,0:T(8,128)}, u32[]{:S(2)}) copy-start(f32[1,64,512]{2,1,0:T(8,128)} %reduce-scatter.9.cloned.1.call-done) | copy-start | bytes 393220
  775.5 1460.8 %copy-start.52 = (f32[1,64,512]{2,1,0:T(8,128)S(1)}, f32[1,64,512]{2,1,0:T(8,128)}, u32[]{:S(2)}) copy-start(f32[1,64,512]{2,1,0:T(8,128)} %param.33) | copy-start | bytes 393220
  775.5 1460.8 %copy-start.53 = (f32[1,64,512]{2,1,0:T(8,128)S(1)}, f32[1,64,512]{2,1,0:T(8,128)}, u32[]{:S(2)}) copy-start(f32[1,64,512]{2,1,0:T(8,128)} %param.39) | copy-start | bytes 393220
  1103.1 1134.0 %copy-start.35 = (f32[1,64,1536]{2,1,0:T(8,128)S(1)}, f32[1,64,1536]{2,1,0:T(8,128)}, u32[]{:S(2)}) copy-start(f32[1,64,1536]{2,1,0:T(8,128)} %param.26) | copy-start | bytes 1179652
  1103.1 1134.0 %copy-start.36 = (f32[1,64,1536]{2,1,0:T(8,128)S(1)}, f32[1,64,1536]{2,1,0:T(8,128)}, u32[]{:S(2)}) copy-start(f32[1,64,1536]{2,1,0:T(8,128)} %reduce-scatter.7.cloned.1.call-done) | copy-start | bytes 1179652
  2188.7 50.9 %copy-start.27 = (f32[1,64,2048]{2,1,0:T(8,128)S(1)}, f32[1,64,2048]{2,1,0:T(8,128)}, u32[]{:S(2)}) copy-start(f32[1,64,2048]{2,1,0:T(8,128)} %param.29) | copy-start | bytes 1572868
  2188.7 50.9 %copy-start.30 = (f32[1,64,2048]{2,1,0:T(8,128)S(1)}, f32[1,64,2048]{2,1,0:T(8,128)}, u32[]{:S(2)}) copy-start(f32[1,64,2048]{2,1,0:T(8,128)} %reduce-scatter.13.cloned.1.call-done) | copy-start | bytes 1572868
  2188.7 50.9 %copy-start.42 = (f32[1,64,2048]{2,1,0:T(8,128)S(1)}, f32[1,64,2048]{2,1,0:T(8,128)}, u32[]{:S(2)}) copy-start(f32[1,64,2048]{2,1,0:T(8,128)} %param.35) | copy-start | bytes 1572868
  2188.7 50.9 %copy-start.43 = (f32[1,64,2048]{2,1,0:T(8,128)S(1)}, f32[1,64,2048]{2,1,0:T(8,128)}, u32[]{:S(2)}) copy-start(f32[1,64,2048]{2,1,0:T(8,128)} %param.41) | copy-start | bytes 1572868
  2237.1 4.0 copy-start.45
  2237.1 5.5 copy-start.39
  2239.7 5.1 copy-start.32
  (54 other events, 116.0 us)
Sparse Core Ops, SparseCore 0:
  11.3 85.4 all-gather.6
  100.1 190.1 all-gather.8
  293.7 66.3 all-gather.10
  363.3 53.7 all-gather.12
  419.9 18.3 all-reduce.5
  442.0 77.2 all-gather.14
  523.0 74.6 all-gather.16
  602.9 17.3 all-reduce.7
  634.3 19.8 all-reduce.9
  669.5 19.9 all-reduce.11
  692.3 81.5 reduce-scatter.8
  779.1 142.9 reduce-scatter.6
  924.3 176.9 reduce-scatter.10
  1103.4 180.1 reduce-scatter.12
  1285.8 211.6 reduce-scatter.16
  1499.7 686.1 reduce-scatter.14
where the time goes:
time: 2270 us; the launch traced here: 2260 us
  waiting for transfers between devices  2020 us (89%)
  matrix products  81.6 us (4%)
  other arithmetic  65.1 us (3%)
  blocking collectives  44.8 us (2%)
  between operations  25.2 us (1%)
  local copies, waits for them, and re-layouts  24.5 us (1%)
    reduce_scatter x1, waiting for transfers between devices, local(): lax.psum_scatter(grad_modulation, 'dp', scatter_dimension=0, tiled=True)  687 us
    reduce_scatter x1, waiting for transfers between devices, local(): lax.psum_scatter(grad_embedding, 'dp', scatter_dimension=1, tiled=True)  211 us
    all_gather x1, waiting for transfers between devices, local(): lax.all_gather(local_modulation, 'dp', axis=0, tiled=True)  184 us
    reduce_scatter x1, waiting for transfers between devices, local(): lax.psum_scatter(grad_hidden_out, 'dp', scatter_dimension=1, tiled=True)  180 us
    reduce_scatter x1, waiting for transfers between devices, local(): lax.psum_scatter(grad_hidden_in, 'dp', scatter_dimension=1, tiled=True)  176 us
    reduce_scatter x1, waiting for transfers between devices, local(): lax.psum_scatter(grad_attend_in, 'dp', scatter_dimension=1, tiled=True)  146 us
    all_gather x1, waiting for transfers between devices, local(): lax.all_gather(embedding.astype(jnp.bfloat16), 'dp', axis=1, tiled=True)  79.3 us
    all_gather x1, waiting for transfers between devices, local(): lax.all_gather(hidden_in.astype(jnp.bfloat16), 'dp', axis=1, tiled=True)  78.8 us
  transfers between devices with their start and end apart: 16, of which 15 were waited for; matrix products, arithmetic and copies ran while one was open for 5% of the time, Pallas kernels for 0%

commit v1 on v0

v1 whole, which is shorter than its diff:
```python
from functools import partial
import math

import jax
import jax.numpy as jnp
from jax import lax
from jax.sharding import PartitionSpec as P

D = 1024
HEAD = 64
FREQ = 256
CLASSES = 1001
GRID = 16
LAYERS = 1
STEP = 10
OUT = 32

LN_EPS = 1e-06
BETA_ONE = 0.5
BETA_TWO = 0.5
LEARN_RATE = 0.01
DECAY_RATE = 0.1
ADAM_EPS = 1e-08
CLIP_SCALE = 40.0
NORM_EPS = 1e-06

BF = jnp.bfloat16
F32 = jnp.float32


def mm(a, b):
    return jnp.dot(a, b, preferred_element_type=F32)


def mm_tn(a, b):
    return lax.dot_general(a, b, (((0,), (0,)), ((), ())), preferred_element_type=F32)


def mm_nt(a, b):
    return lax.dot_general(a, b, (((1,), (1,)), ((), ())), preferred_element_type=F32)


def to_x(v):
    return lax.ppermute(v, "dp", [(i, i ^ 1) for i in range(16)])


def to_y(v):
    return lax.ppermute(v, "dp", [(i, i ^ 2) for i in range(16)])


def z_up(v):
    return lax.ppermute(v, "dp", [(i, (i + 4) % 16) for i in range(16)])


def z_down(v):
    return lax.ppermute(v, "dp", [(i, (i - 4) % 16) for i in range(16)])


def cores(v):
    return lax.ppermute(v, "tensor", [(0, 1), (1, 0)])


def core_sum(v):
    return v + cores(v)


def relative_order(n):
    here = lax.axis_index("dp")
    k = jnp.arange(n, dtype=jnp.int32)
    if n != 16:
        return k, k
    z, y, x = here // 4, (here // 2) % 2, here % 2
    ky, kx, kz = k // 8, (k // 4) % 2, k % 4
    order = ((z - kz) % 4) * 4 + (y ^ ky) * 2 + (x ^ kx)
    zb, yb, xb = k // 4, (k // 2) % 2, k % 2
    place = (yb ^ y) * 8 + (xb ^ x) * 4 + (z - zb) % 4
    return order, place


def gather_z_first(shard):
    half = shard.shape[1] // 2
    ring = [shard]
    for _ in range(3):
        ring.append(z_up(ring[-1]))
    left = jnp.concatenate([b[:, :half] for b in ring], axis=0)
    right = jnp.concatenate([b[:, half:] for b in ring], axis=0)
    lx, ly = to_x(left), to_y(left)
    ry, rx = to_y(right), to_x(right)
    lxy, rxy = to_y(lx), to_x(ry)
    return jnp.concatenate(
        [
            jnp.concatenate([left, lx, ly, lxy], axis=0),
            jnp.concatenate([right, rx, ry, rxy], axis=0),
        ],
        axis=1,
    )


def gather_z_last(shard):
    r, c = shard.shape
    pair = jnp.stack([shard, to_x(shard)])
    quad = jnp.concatenate([pair, to_y(pair)])
    ring = [quad]
    for _ in range(3):
        ring.append(z_up(ring[-1]))
    return jnp.stack(ring, axis=1).reshape(16 * r, c)


def scatter_z_last(grad):
    rows, c = grad.shape
    quad, r, half = rows // 4, rows // 16, c // 2
    q = [grad[k * quad : (k + 1) * quad] for k in range(4)]
    lq = [v[:, :half] for v in q]
    rq = [v[:, half:] for v in q]
    l2, l3 = to_y(lq[2].astype(BF)), to_y(lq[3].astype(BF))
    r1, r3 = to_x(rq[1].astype(BF)), to_x(rq[3].astype(BF))
    ls = lq[0] + l2.astype(F32)
    rs = rq[0] + r1.astype(F32)
    lt = to_x((lq[1] + l3.astype(F32)).astype(BF))
    rt = to_y((rq[2] + r3.astype(F32)).astype(BF))
    s = jnp.concatenate([ls + lt.astype(F32), rs + rt.astype(F32)], axis=1)
    total = s[3 * r :]
    for k in (2, 1, 0):
        total = s[k * r : (k + 1) * r] + z_down(total.astype(BF)).astype(F32)
    return total


def scatter_z_first(grad):
    rows, c = grad.shape
    r = rows // 16
    g = grad.reshape(4, 4, r, c)
    total = g[:, 3]
    for k in (2, 1, 0):
        total = g[:, k] + z_down(total.astype(BF)).astype(F32)
    pair = total[:2] + to_y(total[2:].astype(BF)).astype(F32)
    return pair[0] + to_x(pair[1].astype(BF)).astype(F32)


def exchange(v):
    return lax.all_to_all(v, "dp", 0, 0, tiled=True)


def everyone(v):
    return exchange(jnp.broadcast_to(v[None], (lax.axis_size("dp"),) + v.shape))


def normalize(v):
    center = v - jnp.mean(v, axis=-1, keepdims=True)
    inv = lax.rsqrt(jnp.mean(center * center, axis=-1, keepdims=True) + LN_EPS)
    return center * inv, inv


def modulate_back(normed, inv, scale, d):
    e = d * (1.0 + scale)
    dv = inv * (
        e
        - jnp.mean(e, axis=-1, keepdims=True)
        - normed * jnp.mean(e * normed, axis=-1, keepdims=True)
    )
    return dv, jnp.sum(d, axis=0), jnp.sum(d * normed, axis=0)


def silu_back(v, d):
    _, pullback = jax.vjp(jax.nn.silu, v)
    return pullback(d)[0]


def gelu_back(v, d):
    _, pullback = jax.vjp(partial(jax.nn.gelu, approximate=True), v)
    return pullback(d)[0]


def time_table(step_values):
    half_count = FREQ // 2
    rates = jnp.exp(-math.log(10000.0) * jnp.arange(half_count, dtype=F32) / half_count)
    angles = step_values.astype(F32)[:, None] * rates[None, :]
    return jnp.concatenate([jnp.cos(angles), jnp.sin(angles)], axis=1)


def position_table(order):
    quarter = D // 4
    width = D // order.shape[0]
    feature = (order[:, None] * width + jnp.arange(width, dtype=jnp.int32)[None, :]).reshape(1, D)
    rates = 1.0 / 10000.0 ** ((feature % quarter).astype(F32) / quarter)
    angles = jnp.arange(GRID, dtype=F32)[:, None] * rates
    part = feature // quarter
    table = jnp.where(part % 2 == 0, jnp.sin(angles), jnp.cos(angles))
    both = jnp.where(part < 2, table[None, :, :], table[:, None, :])
    return both.reshape(GRID * GRID, D)


def adam_update(master, moment, square, gradient, factor):
    clipped = gradient * factor
    new_moment = BETA_ONE * moment + (1.0 - BETA_ONE) * clipped
    new_square = BETA_TWO * square + (1.0 - BETA_TWO) * clipped * clipped
    first_hat = new_moment / (1.0 - BETA_ONE**STEP)
    second_hat = new_square / (1.0 - BETA_TWO**STEP)
    change = -LEARN_RATE * (first_hat / (jnp.sqrt(second_hat) + ADAM_EPS) + DECAY_RATE * master)
    return (change, new_moment, new_square)


def attend_forward(packed):
    q, k, v = packed[:, :, 0], packed[:, :, 1], packed[:, :, 2]
    scores = jnp.einsum("qhe,khe->hqk", q, k, preferred_element_type=F32) * HEAD ** (-0.5)
    prob = jax.nn.softmax(scores, axis=-1)
    mixture = jnp.einsum("hqk,khe->qhe", prob.astype(BF), v, preferred_element_type=F32)
    return prob, mixture.astype(BF)


def attend_back(packed, prob, d_mix):
    q, k, v = packed[:, :, 0], packed[:, :, 1], packed[:, :, 2]
    dv = jnp.einsum("hqk,qhe->khe", prob.astype(BF), d_mix, preferred_element_type=F32)
    dp = jnp.einsum("qhe,khe->hqk", d_mix, v, preferred_element_type=F32)
    ds = (prob * (dp - jnp.sum(prob * dp, axis=-1, keepdims=True))).astype(BF)
    dq = jnp.einsum("hqk,khe->qhe", ds, k, preferred_element_type=F32) * HEAD ** (-0.5)
    dk = jnp.einsum("hqk,qhe->khe", ds, q, preferred_element_type=F32) * HEAD ** (-0.5)
    return jnp.stack([dq, dk, dv], axis=2).astype(BF)


def local(
    patches,
    timesteps,
    labels,
    target,
    attend_in,
    attend_out,
    hidden_in,
    hidden_out,
    modulation,
    embedding,
    *moments_squares,
):
    n = lax.axis_size("dp")
    images, length, patch_width = patches.shape
    assert images == 1
    tokens_all = length * n
    entries = tokens_all * OUT
    order, place = relative_order(n)
    cols = D // n

    rows_two = patch_width + FREQ
    rows_class = rows_two + D
    rows_head = rows_class + CLASSES
    emb = embedding.astype(BF)
    time_two = emb[rows_two:rows_class]
    class_table = emb[rows_class:rows_head]

    w_ai, w_ao = attend_in[0].astype(BF), attend_out[0].astype(BF)
    w_hi, w_ho = hidden_in[0].astype(BF), hidden_out[0].astype(BF)
    ai_cols, ao_cols, ff = w_ai.shape[1], w_ao.shape[1], w_hi.shape[1]
    ai_half, ao_half = ai_cols // 2, ao_cols // 2
    g_small = jnp.concatenate([emb[:rows_two], emb[rows_head:]], axis=0).T
    g_one = jnp.concatenate(
        [w_ai[:, :ai_half], w_ao[:, :ao_half], w_ai[:, ai_half:], w_ao[:, ao_half:]], axis=1
    )
    if n == 16:
        small = gather_z_last(g_small)
        one = gather_z_first(g_one)
        full_hi = gather_z_first(w_hi)
        full_ho = jnp.concatenate(
            [gather_z_first(w_ho[:, : ff // 2]), gather_z_last(w_ho[:, ff // 2 :])], axis=1
        )
    else:
        small, one, full_hi, full_ho = [
            lax.all_gather(v, "dp", axis=0, tiled=True) for v in (g_small, g_one, w_hi, w_ho)
        ]
    mid = ai_half + ao_half
    full_ai = jnp.concatenate([one[:, :ai_half], one[:, mid : mid + ai_half]], axis=1)
    full_ao = jnp.concatenate([one[:, ai_half:mid], one[:, mid + ai_half :]], axis=1)
    patch_t = small[:, :patch_width]
    time_t = small[:, patch_width:rows_two]
    head_t = small[:, rows_two:]

    codes = everyone(jnp.concatenate([timesteps, labels]))
    steps, marks = codes[:, 0], codes[:, 1]
    frequencies = time_table(steps).astype(BF)
    time_pre_rel = mm_nt(frequencies, time_t)
    time_pre = jnp.take(time_pre_rel.reshape(n, n, cols), place, axis=1).reshape(n, D)
    time_act = jax.nn.silu(time_pre).astype(BF)
    one_hot = marks[:, None] == jnp.arange(CLASSES, dtype=jnp.int32)[None, :]
    condition = mm(time_act, time_two) + mm(one_hot.astype(BF), class_table)
    cond_own = jax.nn.silu(condition).astype(BF)
    cond_act = jnp.swapaxes(everyone(cond_own), 0, 1).reshape(n, D)
    modulation_low = modulation.astype(BF)
    mods = exchange(mm_nt(cond_act, modulation_low)).reshape(8, n, cols)
    mods = jnp.take(mods, order, axis=1).reshape(8, D)
    shift_one, scale_one, gate_one, shift_two, scale_two, gate_two, shift_end, scale_end = [
        mods[k][None] for k in range(8)
    ]

    tokens = patches[0]
    x_in = mm_nt(tokens, patch_t) + position_table(order)
    n_one, inv_one = normalize(x_in)
    h_one = (n_one * (1.0 + scale_one) + shift_one).astype(BF)
    heads = ai_cols // (3 * HEAD)
    packed = mm(h_one, full_ai).astype(BF).reshape(length, heads, 3, HEAD)
    prob, mixture = attend_forward(packed)
    mixture = mixture.reshape(length, heads * HEAD)
    branch_one = core_sum(mm_nt(mixture, full_ao))
    x_mid = x_in + gate_one * branch_one
    n_two, inv_two = normalize(x_mid)
    h_two = (n_two * (1.0 + scale_two) + shift_two).astype(BF)
    inner = mm(h_two, full_hi)
    active = jax.nn.gelu(inner, approximate=True).astype(BF)
    part = mm_nt(active, full_ho).astype(BF)
    branch_two = part.astype(F32) + cores(part).astype(F32)
    x_end = x_mid + gate_two * branch_two
    n_end, inv_end = normalize(x_end)
    h_end = (n_end * (1.0 + scale_end) + shift_end).astype(BF)
    output = mm(h_end, head_t)
    residue = output - target[0]
    local_loss = jnp.sum(residue * residue)

    d_out = (residue * (2.0 / entries)).astype(BF)
    d_head = mm_tn(h_end, d_out)
    dx, d_shift_end, d_scale_end = modulate_back(n_end, inv_end, scale_end, mm_nt(d_out, head_t))
    d_gate_two = jnp.sum(dx * branch_two, axis=0)
    d_two = (gate_two * dx).astype(BF)
    d_ho = mm_tn(d_two, active)
    d_inner = gelu_back(inner, mm(d_two, full_ho)).astype(BF)
    d_hi = mm_tn(h_two, d_inner)
    part = mm_nt(d_inner, full_hi).astype(BF)
    d_h_two = part.astype(F32) + cores(part).astype(F32)
    dv, d_shift_two, d_scale_two = modulate_back(n_two, inv_two, scale_two, d_h_two)
    dx = dx + dv
    d_gate_one = jnp.sum(dx * branch_one, axis=0)
    d_one = (gate_one * dx).astype(BF)
    d_ao = mm_tn(d_one, mixture)
    d_mix = mm(d_one, full_ao).astype(BF).reshape(length, heads, HEAD)
    d_packed = attend_back(packed, prob, d_mix).reshape(length, ai_cols)
    d_ai = mm_tn(h_one, d_packed)
    part = mm_nt(d_packed, full_ai).astype(BF)
    d_h_one = part.astype(F32) + cores(part).astype(F32)
    dv, d_shift_one, d_scale_one = modulate_back(n_one, inv_one, scale_one, d_h_one)
    dx = (dx + dv).astype(BF)
    d_patch = mm_tn(dx, tokens)

    d_g_one = jnp.concatenate(
        [d_ai[:, :ai_half], d_ao[:, :ao_half], d_ai[:, ai_half:], d_ao[:, ao_half:]], axis=1
    )
    if n == 16:
        own_ho = jnp.concatenate(
            [scatter_z_last(d_ho[:, : ff // 2]), scatter_z_first(d_ho[:, ff // 2 :])], axis=1
        )
        own_hi = scatter_z_last(d_hi)
        own_one = scatter_z_last(d_g_one)
    else:
        own_ho, own_hi, own_one = [
            lax.psum_scatter(v, "dp", scatter_dimension=0, tiled=True) for v in (d_ho, d_hi, d_g_one)
        ]
    own_ai = jnp.concatenate([own_one[:, :ai_half], own_one[:, mid : mid + ai_half]], axis=1)
    own_ao = jnp.concatenate([own_one[:, ai_half:mid], own_one[:, mid + ai_half :]], axis=1)
    d_ends = jnp.concatenate([d_patch, d_head], axis=1).reshape(n, cols, patch_width + OUT)
    own_ends = jnp.sum(exchange(jnp.take(d_ends, place, axis=0)), axis=0).T

    d_mods = jnp.stack(
        [
            d_shift_one,
            d_scale_one,
            d_gate_one,
            d_shift_two,
            d_scale_two,
            d_gate_two,
            d_shift_end,
            d_scale_end,
        ]
    )
    d_mods = jnp.take(d_mods.reshape(8, n, cols), place, axis=1).reshape(n, -1).astype(BF)
    d_mods = exchange(d_mods)
    own_modulation = mm_tn(d_mods, cond_act)
    d_cond = mm(d_mods, modulation_low)
    d_cond = jnp.sum(exchange(jnp.swapaxes(d_cond.reshape(n, n, cols), 0, 1)), axis=0)
    d_cond = silu_back(condition, d_cond)
    own_class = lax.dot_general(
        one_hot.astype(F32),
        d_cond,
        (((0,), (0,)), ((), ())),
        precision=lax.Precision.HIGHEST,
        preferred_element_type=F32,
    )
    d_temb = d_cond.astype(BF)
    own_time_two = mm_tn(time_act, d_temb)
    d_time = mm_nt(d_temb, time_two)
    d_time = jnp.sum(exchange(jnp.swapaxes(d_time.reshape(n, n, cols), 0, 1)), axis=0)
    d_time_pre = silu_back(time_pre_rel[:, :cols] if n == 16 else lax.dynamic_slice_in_dim(time_pre, lax.axis_index("dp") * cols, cols, 1), d_time).astype(BF)
    own_time_one = mm_tn(frequencies, d_time_pre)
    own_embedding = jnp.concatenate(
        [own_ends[:patch_width], own_time_one, own_time_two, own_class, own_ends[patch_width:]], axis=0
    )

    owned = (own_ai[None], own_ao[None], own_hi[None], own_ho[None], own_modulation, own_embedding)
    sums = [jnp.sum(g * g) for g in owned]
    split_square = sums[0] + sums[1] + sums[2] + sums[3]
    shared_square = sums[4] + sums[5]
    totals = jnp.stack([local_loss * 0.5, split_square + 0.5 * shared_square])
    if n == 16:
        totals = core_sum(totals)
        for hop in (1, 2, 4, 8):
            totals = totals + lax.ppermute(totals, "dp", [(i, i ^ hop) for i in range(16)])
    else:
        totals = lax.psum(totals, ("dp", "tensor"))
    loss_value = totals[0] / entries
    prenorm = jnp.sqrt(totals[1])
    factor = jnp.minimum(1.0, CLIP_SCALE / math.sqrt(tokens_all) / (prenorm + NORM_EPS))
    masters = (attend_in, attend_out, hidden_in, hidden_out, modulation, embedding)
    moments, squares = moments_squares[:6], moments_squares[6:]
    results = [
        adam_update(masters[s], moments[s], squares[s], owned[s], factor) for s in range(6)
    ]
    return (loss_value, prenorm) + tuple(results[s][part] for part in range(3) for s in range(6))


def solution(mesh):
    weights = (P(None, "dp", "tensor"),) * 4 + (P("dp", None), P(None, "dp"))
    return jax.shard_map(
        local,
        mesh=mesh,
        in_specs=(P("dp", None, None), P("dp"), P("dp"), P("dp", None, None)) + weights * 3,
        out_specs=(P(), P()) + weights * 3,
        check_vma=False,
    )
```

time: 2270 us -> 529 us (0.23)
  waiting for transfers between devices: 2020 us -> 133 us
  starting transfers between devices: 1.3 us -> 145 us
  local copies, waits for them, and re-layouts: 24.5 us -> 96.5 us
  blocking collectives: 44.8 us -> 0 us
  matrix products: 81.6 us -> 48.3 us
  other arithmetic: 65.1 us -> 88.5 us
    reduce_scatter x6 -> x0, waiting for transfers between devices: 1440 us -> none  [the longest x1 687 us: local(): lax.psum_scatter(grad_modulation, 'dp', scatter_dimension=0, tiled=True)]
    all_gather x6 -> x0, waiting for transfers between devices: 528 us -> none  [the longest x1 184 us: local(): lax.all_gather(local_modulation, 'dp', axis=0, tiled=True)]
    ppermute x0 -> x78, waiting for transfers between devices: none -> 115 us  [the longest x21 33.6 us: to_y(): return lax.ppermute(v, 'dp', [(i, i ^ 2) for i in range(16)])]
    ppermute x0 -> x78, starting transfers between devices: none -> 111 us  [the longest x12 32.3 us: z_down(): return lax.ppermute(v, 'dp', [(i, (i - 4) % 16) for i in range(16)])]
    psum x4 -> x0, waiting for transfers between devices: 52.9 us -> none  [the longest x1 19.8 us: local(): lax.psum(times_right_t(grad_inner, full_hidden_in[layer_index]).astype(jn...]
    psum x1 -> x0, blocking collectives: 44.8 us -> none  [local(): lax.psum((local_loss * 0.5, split_square + 0.5 * shared_square), ('dp', '...]
    dot_general x29 -> x32, matrix products: 81.6 us -> 45.1 us  [the longest x9 15.7 us: mm_tn(): lax.dot_general(a, b, (((0,), (0,)), ((), ())), preferred_element_type=F32)]
    all_to_all x0 -> x7, starting transfers between devices: none -> 33.9 us  [exchange(): return lax.all_to_all(v, 'dp', 0, 0, tiled=True)]
  transfers between devices with their start and end apart: 16 -> 85, of which waited for: 15 -> 31; matrix products, arithmetic and copies ran while one was open for 5% -> 34% of each run, Pallas kernels for 0% -> 0%
where the time goes in v1:
time: 529 us; the launch traced here: 524 us
  starting transfers between devices  145 us (27%)
  waiting for transfers between devices  133 us (25%)
  local copies, waits for them, and re-layouts  96.5 us (18%)
  other arithmetic  88.5 us (17%)
  matrix products  48.3 us (9%)
  between operations  12.6 us (2%)
    unnamed x263, local copies, waits for them, and re-layouts  34.2 us
    all_to_all x7, starting transfers between devices, exchange(): return lax.all_to_all(v, 'dp', 0, 0, tiled=True)  33.9 us
    ppermute x21, waiting for transfers between devices, to_y(): return lax.ppermute(v, 'dp', [(i, i ^ 2) for i in range(16)])  33.6 us
    ppermute x12, starting transfers between devices, z_down(): return lax.ppermute(v, 'dp', [(i, (i - 4) % 16) for i in range(16)])  32.3 us
    ppermute x21, waiting for transfers between devices, to_x(): return lax.ppermute(v, 'dp', [(i, i ^ 1) for i in range(16)])  31.1 us
    ppermute x15, starting transfers between devices, z_up(): return lax.ppermute(v, 'dp', [(i, (i + 4) % 16) for i in range(16)])  26.5 us
    ppermute x21, starting transfers between devices, to_y(): return lax.ppermute(v, 'dp', [(i, i ^ 2) for i in range(16)])  25.4 us
    ppermute x21, starting transfers between devices, to_x(): return lax.ppermute(v, 'dp', [(i, i ^ 1) for i in range(16)])  22.3 us
  transfers between devices with their start and end apart: 85, of which 31 were waited for; matrix products, arithmetic and copies ran while one was open for 34% of the time, Pallas kernels for 0%

profile of v1, /device:TPU:0, one launch (start us, length us, event | category | flops | bytes accessed | tf_op | source)
XLA Modules:
  0.0 524.0 jit_solution(10687585111780115654)
XLA Ops:
  2.8 8.3 %all-to-all-start = ((s32[16,1,2]{2,1,0:T(1,128)}), s32[16,1,2]{2,1,0:T(1,128)S(1)}, u32[]{:S(2)}, u32[]{:S(2)}) async-start(s32[16,1,2]{2,1,0:T(1,128)} %broadcast_in_dim.117), calls=%async_computation | async-start | bytes 16384 | tf_op jit(solution)/shard_map/all_to_all | solution.py:140
  34.8 3.0 collective-permute-done.1
  46.8 4.0 collective-permute-done.25
  55.1 8.7 %collective-permute-done.26 = bf16[64,1024]{1,0:T(8,128)(2,1)S(1)} collective-permute-done((bf16[64,1024]{1,0:T(8,128)(2,1)S(1)}, bf16[64,1024]{1,0:T(8,128)(2,1)S(1)}, u32[]{:S(2)}, u32[]{:S(2)}) %collective-permute-start.26) | collective-permute-done | bytes 131104 | tf_op jit(solution)/shard_map/ppermute | solution.py:52
  73.6 8.6 %collective-permute-done.4 = bf16[4,64,304]{2,1,0:T(8,128)(2,1)S(1)} collective-permute-done((bf16[4,64,304]{2,1,0:T(8,128)(2,1)S(1)}, bf16[4,64,304]{2,1,0:T(8,128)(2,1)S(1)}, u32[]{:S(2)}, u32[]{:S(2)}) %collective-permute-start.4) | collective-permute-done | bytes 155680 | tf_op jit(solution)/shard_map/ppermute | solution.py:52
  86.2 6.1 %all-to-all-start.1 = ((bf16[16,2,512]{2,1,0:T(2,128)(2,1)}), bf16[16,2,512]{2,1,0:T(2,128)(2,1)S(1)}, u32[]{:S(2)}, u32[]{:S(2)}) async-start(bf16[16,2,512]{2,1,0:T(2,128)(2,1)} %reshape.1026), calls=%async_computation.1 | async-start | bytes 65536 | tf_op jit(solution)/shard_map/all_to_all | solution.py:140
  95.2 4.6 all-to-all-done.1
  101.6 4.1 all-to-all-start.2
  142.6 4.7 collective-permute-done.12
  150.9 6.0 %collective-permute-done.8 = bf16[256,1024]{1,0:T(8,128)(2,1)S(1)} collective-permute-done((bf16[256,1024]{1,0:T(8,128)(2,1)S(1)}, bf16[256,1024]{1,0:T(8,128)(2,1)S(1)}, u32[]{:S(2)}, u32[]{:S(2)}) %collective-permute-start.8) | collective-permute-done | bytes 524320 | tf_op jit(solution)/shard_map/ppermute | solution.py:44
  160.0 8.2 %collective-permute-done.13 = bf16[256,1024]{1,0:T(8,128)(2,1)S(1)} collective-permute-done((bf16[256,1024]{1,0:T(8,128)(2,1)S(1)}, bf16[256,1024]{1,0:T(8,128)(2,1)S(1)}, u32[]{:S(2)}, u32[]{:S(2)}) %collective-permute-start.13) | collective-permute-done | bytes 524320 | tf_op jit(solution)/shard_map/ppermute | solution.py:44
  170.6 12.1 %collective-permute-start.36 = (bf16[4,64,1024]{2,1,0:T(8,128)(2,1)}, bf16[4,64,1024]{2,1,0:T(8,128)(2,1)}, u32[]{:S(2)}, u32[]{:S(2)}) collective-permute-start(bf16[4,64,1024]{2,1,0:T(8,128)(2,1)} %collective-permute-done.35), channel_id=1, source_target_pairs={{0,8},{2,10},{4,12},{6,14},{8,16},{10,18},{12,20},{14,22},{16,24},... | collective-permute-start | bytes 1572872 | tf_op jit(solution)/shard_map/ppermute | solution.py:52
  188.5 3.2 fusion.235
  203.2 5.5 %collective-permute-done.19 = bf16[256,1024]{1,0:T(8,128)(2,1)S(1)} collective-permute-done((bf16[256,1024]{1,0:T(8,128)(2,1)}, bf16[256,1024]{1,0:T(8,128)(2,1)S(1)}, u32[]{:S(2)}, u32[]{:S(2)}) %collective-permute-start.19) | collective-permute-done | bytes 524320 | tf_op jit(solution)/shard_map/ppermute | solution.py:48
  208.9 6.8 %collective-permute-done.20 = bf16[256,1024]{1,0:T(8,128)(2,1)S(1)} collective-permute-done((bf16[256,1024]{1,0:T(8,128)(2,1)}, bf16[256,1024]{1,0:T(8,128)(2,1)S(1)}, u32[]{:S(2)}, u32[]{:S(2)}) %collective-permute-start.20) | collective-permute-done | bytes 524320 | tf_op jit(solution)/shard_map/ppermute | solution.py:48
  230.2 2.6 copy.181
  237.0 4.1 fusion.11
  244.6 5.1 fusion.236
  263.2 7.8 %collective-permute-done.62 = bf16[256,512]{1,0:T(8,128)(2,1)} collective-permute-done((bf16[256,512]{1,0:T(8,128)(2,1)}, bf16[256,512]{1,0:T(8,128)(2,1)}, u32[]{:S(2)}, u32[]{:S(2)}) %collective-permute-start.62) | collective-permute-done | bytes 262176 | tf_op jit(solution)/shard_map/ppermute | solution.py:44
  296.0 5.0 collective-permute-done.53
  306.7 3.2 collective-permute-done.63
  314.0 3.9 collective-permute-done.60
  322.3 3.5 collective-permute-done.64
  328.9 2.4 collective-permute-start.68
  336.5 4.3 all-to-all-start.3
  358.4 5.2 collective-permute-done.54
  363.7 3.6 collective-permute-start.65
  367.3 3.4 fusion.44
  370.7 4.2 collective-permute-done.41
  378.3 3.3 collective-permute-start.66
  386.1 3.5 all-to-all-start.5
  392.5 4.7 all-to-all-done.5
  405.1 3.5 all-to-all-start.6
  410.4 5.7 %all-to-all-done.6 = f32[16,1,1024]{2,1,0:T(1,128)S(1)} async-done(((f32[16,1,1024]{2,1,0:T(1,128)}), f32[16,1,1024]{2,1,0:T(1,128)S(1)}, u32[]{:S(2)}, u32[]{:S(2)}) %all-to-all-start.6) | async-done | bytes 65568 | tf_op jit(solution)/shard_map/all_to_all | solution.py:140
  416.1 4.2 all-to-all-start.4
  425.4 3.1 all-to-all-done.4
  428.4 2.7 reduce.36
  445.8 8.5 %collective-permute-done.69 = bf16[4,64,1024]{2,1,0:T(8,128)(2,1)S(1)} collective-permute-done((bf16[4,64,1024]{2,1,0:T(8,128)(2,1)}, bf16[4,64,1024]{2,1,0:T(8,128)(2,1)S(1)}, u32[]{:S(2)}, u32[]{:S(2)}) %collective-permute-start.69) | collective-permute-done | bytes 524320 | tf_op jit(solution)/shard_map/ppermute | solution.py:56
  457.2 3.4 collective-permute-start.55
  460.6 3.0 collective-permute-start.47
  464.2 2.6 collective-permute-done.55
  466.8 4.3 collective-permute-start.56
  475.8 4.5 collective-permute-start.57
  489.8 3.3 collective-permute-done.74
  496.8 3.5 collective-permute-done.76
  500.3 2.8 collective-permute-start.77
  508.6 2.7 add_multiply_fusion.4
  517.4 4.1 add_multiply_fusion
  (632 shorter events, 285.7 us)
Async XLA Ops:
  2.8 29.4 %all-to-all-start = ((s32[16,1,2]{2,1,0:T(1,128)}), s32[16,1,2]{2,1,0:T(1,128)S(1)}, u32[]{:S(2)}, u32[]{:S(2)}) async-start(s32[16,1,2]{2,1,0:T(1,128)} %broadcast_in_dim.117), calls=%async_computation | async-start | bytes 16384 | tf_op jit(solution)/shard_map/all_to_all | solution.py:140
  13.8 30.0 %collective-permute-start.5 = (bf16[64,2048]{1,0:T(8,128)(2,1)}, bf16[64,2048]{1,0:T(8,128)(2,1)}, u32[]{:S(2)}, u32[]{:S(2)}) collective-permute-start(bf16[64,2048]{1,0:T(8,128)(2,1)} %pad_maximum_fusion.35), channel_id=1, source_target_pairs={{0,8},{2,10},{4,12},{6,14},{8,16},{10,18},{12,20},{14,22},{16,24},... | collective-permute-start | bytes 786440 | tf_op jit(solution)/shard_map/ppermute | solution.py:52
  15.8 29.5 %collective-permute-start.15 = (bf16[64,2048]{1,0:T(8,128)(2,1)S(1)}, bf16[64,2048]{1,0:T(8,128)(2,1)}, u32[]{:S(2)}, u32[]{:S(2)}) collective-permute-start(bf16[64,2048]{1,0:T(8,128)(2,1)S(1)} %convert_bitcast_fusion.1), channel_id=1, source_target_pairs={{0,8},{2,10},{4,12},{6,14},{8,16},{10,18},{12,20},{14,22},{16,24},... | collective-permute-start | bytes 786440 | tf_op jit(solution)/shard_map/ppermute | solution.py:52
  20.4 20.4 %collective-permute-start.24 = (bf16[64,1024]{1,0:T(8,128)(2,1)}, bf16[64,1024]{1,0:T(8,128)(2,1)}, u32[]{:S(2)}, u32[]{:S(2)}) collective-permute-start(bf16[64,1024]{1,0:T(8,128)(2,1)} %get-tuple-element.122), channel_id=1, source_target_pairs={{0,8},{2,10},{4,12},{6,14},{8,16},{10,18},{12,20},{14,22},{16,24},... | collective-permute-start | bytes 393224 | tf_op jit(solution)/shard_map/ppermute | solution.py:52
  21.9 17.0 %collective-permute-start.33 = (bf16[64,1024]{1,0:T(8,128)(2,1)}, bf16[64,1024]{1,0:T(8,128)(2,1)S(1)}, u32[]{:S(2)}, u32[]{:S(2)}) collective-permute-start(bf16[64,1024]{1,0:T(8,128)(2,1)} %get-tuple-element.124), channel_id=1, source_target_pairs={{0,2},{2,0},{4,6},{6,4},{8,10},{10,8},{12,14},{14,12},{16,18},{18,... | collective-permute-start | bytes 393224 | tf_op jit(solution)/shard_map/ppermute | solution.py:44
  38.7 16.4 %collective-permute-start.2 = (bf16[4,64,304]{2,1,0:T(8,128)(2,1)S(1)}, bf16[4,64,304]{2,1,0:T(8,128)(2,1)S(1)}, u32[]{:S(2)}, u32[]{:S(2)}) collective-permute-start(bf16[4,64,304]{2,1,0:T(8,128)(2,1)S(1)} %get-tuple-element.138), channel_id=1, source_target_pairs={{0,8},{2,10},{4,12},{6,14},{8,16},{10,18},{12,20},{14,22},{16,24},... | collective-permute-start | bytes 466952 | tf_op jit(solution)/shard_map/ppermute | solution.py:52
  38.8 27.1 %collective-permute-start.34 = (bf16[2,64,1024]{2,1,0:T(8,128)(2,1)S(1)}, bf16[2,64,1024]{2,1,0:T(8,128)(2,1)S(1)}, u32[]{:S(2)}, u32[]{:S(2)}) collective-permute-start(bf16[2,64,1024]{2,1,0:T(8,128)(2,1)S(1)} %pad_maximum_fusion.38), channel_id=1, source_target_pairs={{0,4},{2,6},{4,0},{6,2},{8,12},{10,14},{12,8},{14,10},{16,20},{18,... | collective-permute-start | bytes 786440 | tf_op jit(solution)/shard_map/ppermute | solution.py:48
  43.9 25.3 %collective-permute-start.6 = (bf16[64,2048]{1,0:T(8,128)(2,1)}, bf16[64,2048]{1,0:T(8,128)(2,1)}, u32[]{:S(2)}, u32[]{:S(2)}) collective-permute-start(bf16[64,2048]{1,0:T(8,128)(2,1)} %collective-permute-done.5), channel_id=1, source_target_pairs={{0,8},{2,10},{4,12},{6,14},{8,16},{10,18},{12,20},{14,22},{16,24},... | collective-permute-start | bytes 786440 | tf_op jit(solution)/shard_map/ppermute | solution.py:52
  45.3 27.4 %collective-permute-start.16 = (bf16[64,2048]{1,0:T(8,128)(2,1)}, bf16[64,2048]{1,0:T(8,128)(2,1)S(1)}, u32[]{:S(2)}, u32[]{:S(2)}) collective-permute-start(bf16[64,2048]{1,0:T(8,128)(2,1)} %collective-permute-done.15), channel_id=1, source_target_pairs={{0,8},{2,10},{4,12},{6,14},{8,16},{10,18},{12,20},{14,22},{16,24},... | collective-permute-start | bytes 786440 | tf_op jit(solution)/shard_map/ppermute | solution.py:52
  55.1 17.1 %collective-permute-start.3 = (bf16[4,64,304]{2,1,0:T(8,128)(2,1)S(1)}, bf16[4,64,304]{2,1,0:T(8,128)(2,1)S(1)}, u32[]{:S(2)}, u32[]{:S(2)}) collective-permute-start(bf16[4,64,304]{2,1,0:T(8,128)(2,1)S(1)} %collective-permute-done.2), channel_id=1, source_target_pairs={{0,8},{2,10},{4,12},{6,14},{8,16},{10,18},{12,20},{14,22},{16,24},... | collective-permute-start | bytes 466952 | tf_op jit(solution)/shard_map/ppermute | solution.py:52
  65.1 40.6 %collective-permute-start.31 = (bf16[256,512]{1,0:T(8,128)(2,1)}, bf16[256,512]{1,0:T(8,128)(2,1)}, u32[]{:S(2)}, u32[]{:S(2)}) collective-permute-start(bf16[256,512]{1,0:T(8,128)(2,1)} %pad_maximum_fusion.37), channel_id=1, source_target_pairs={{0,4},{2,6},{4,0},{6,2},{8,12},{10,14},{12,8},{14,10},{16,20},{18,... | collective-permute-start | bytes 786440 | tf_op jit(solution)/shard_map/ppermute | solution.py:48
  66.0 41.6 %collective-permute-start.30 = (bf16[256,512]{1,0:T(8,128)(2,1)}, bf16[256,512]{1,0:T(8,128)(2,1)}, u32[]{:S(2)}, u32[]{:S(2)}) collective-permute-start(bf16[256,512]{1,0:T(8,128)(2,1)} %pad_maximum_fusion.37), channel_id=1, source_target_pairs={{0,2},{2,0},{4,6},{6,4},{8,10},{10,8},{12,14},{14,12},{16,18},{18,... | collective-permute-start | bytes 786440 | tf_op jit(solution)/shard_map/ppermute | solution.py:44
  69.2 44.9 %collective-permute-start.28 = (bf16[256,512]{1,0:T(8,128)(2,1)}, bf16[256,512]{1,0:T(8,128)(2,1)}, u32[]{:S(2)}, u32[]{:S(2)}) collective-permute-start(bf16[256,512]{1,0:T(8,128)(2,1)} %pad_maximum_fusion.36), channel_id=1, source_target_pairs={{0,4},{2,6},{4,0},{6,2},{8,12},{10,14},{12,8},{14,10},{16,20},{18,... | collective-permute-start | bytes 786440 | tf_op jit(solution)/shard_map/ppermute | solution.py:48
  72.2 40.2 %collective-permute-start.27 = (bf16[256,512]{1,0:T(8,128)(2,1)}, bf16[256,512]{1,0:T(8,128)(2,1)}, u32[]{:S(2)}, u32[]{:S(2)}) collective-permute-start(bf16[256,512]{1,0:T(8,128)(2,1)} %pad_maximum_fusion.36), channel_id=1, source_target_pairs={{0,2},{2,0},{4,6},{6,4},{8,10},{10,8},{12,14},{14,12},{16,18},{18,... | collective-permute-start | bytes 786440 | tf_op jit(solution)/shard_map/ppermute | solution.py:44
  82.2 47.3 %collective-permute-start.7 = (bf16[64,2048]{1,0:T(8,128)(2,1)}, bf16[64,2048]{1,0:T(8,128)(2,1)}, u32[]{:S(2)}, u32[]{:S(2)}) collective-permute-start(bf16[64,2048]{1,0:T(8,128)(2,1)} %collective-permute-done.6), channel_id=1, source_target_pairs={{0,8},{2,10},{4,12},{6,14},{8,16},{10,18},{12,20},{14,22},{16,24},... | collective-permute-start | bytes 786440 | tf_op jit(solution)/shard_map/ppermute | solution.py:52
  105.7 30.5 %collective-permute-start.17 = (bf16[64,2048]{1,0:T(8,128)(2,1)}, bf16[64,2048]{1,0:T(8,128)(2,1)}, u32[]{:S(2)}, u32[]{:S(2)}) collective-permute-start(bf16[64,2048]{1,0:T(8,128)(2,1)} %copy-done.80), channel_id=1, source_target_pairs={{0,8},{2,10},{4,12},{6,14},{8,16},{10,18},{12,20},{14,22},{16,24},... | collective-permute-start | bytes 786440 | tf_op jit(solution)/shard_map/ppermute | solution.py:52
  107.5 33.6 %collective-permute-start.32 = (bf16[256,512]{1,0:T(8,128)(2,1)}, bf16[256,512]{1,0:T(8,128)(2,1)}, u32[]{:S(2)}, u32[]{:S(2)}) collective-permute-start(bf16[256,512]{1,0:T(8,128)(2,1)} %collective-permute-done.31), channel_id=1, source_target_pairs={{0,2},{2,0},{4,6},{6,4},{8,10},{10,8},{12,14},{14,12},{16,18},{18,... | collective-permute-start | bytes 786440 | tf_op jit(solution)/shard_map/ppermute | solution.py:44
  133.9 15.6 %collective-permute-start.11 = (bf16[256,1024]{1,0:T(8,128)(2,1)S(1)}, bf16[256,1024]{1,0:T(8,128)(2,1)S(1)}, u32[]{:S(2)}, u32[]{:S(2)}) collective-permute-start(bf16[256,1024]{1,0:T(8,128)(2,1)S(1)} %pad_maximum_fusion.28), channel_id=1, source_target_pairs={{0,2},{2,0},{4,6},{6,4},{8,10},{10,8},{12,14},{14,12},{16,18},{18,... | collective-permute-start | bytes 1572872 | tf_op jit(solution)/shard_map/ppermute | solution.py:44
  135.6 22.9 %collective-permute-start.9 = (bf16[256,1024]{1,0:T(8,128)(2,1)S(1)}, bf16[256,1024]{1,0:T(8,128)(2,1)S(1)}, u32[]{:S(2)}, u32[]{:S(2)}) collective-permute-start(bf16[256,1024]{1,0:T(8,128)(2,1)S(1)} %pad_maximum_fusion.27), channel_id=1, source_target_pairs={{0,4},{2,6},{4,0},{6,2},{8,12},{10,14},{12,8},{14,10},{16,20},{18,... | collective-permute-start | bytes 1572872 | tf_op jit(solution)/shard_map/ppermute | solution.py:48
  136.2 20.8 %collective-permute-start.8 = (bf16[256,1024]{1,0:T(8,128)(2,1)S(1)}, bf16[256,1024]{1,0:T(8,128)(2,1)S(1)}, u32[]{:S(2)}, u32[]{:S(2)}) collective-permute-start(bf16[256,1024]{1,0:T(8,128)(2,1)S(1)} %pad_maximum_fusion.27), channel_id=1, source_target_pairs={{0,2},{2,0},{4,6},{6,4},{8,10},{10,8},{12,14},{14,12},{16,18},{18,... | collective-permute-start | bytes 1572872 | tf_op jit(solution)/shard_map/ppermute | solution.py:44
  141.1 27.9 %collective-permute-start.35 = (bf16[4,64,1024]{2,1,0:T(8,128)(2,1)S(1)}, bf16[4,64,1024]{2,1,0:T(8,128)(2,1)}, u32[]{:S(2)}, u32[]{:S(2)}) collective-permute-start(bf16[4,64,1024]{2,1,0:T(8,128)(2,1)S(1)} %copy-done.61), channel_id=1, source_target_pairs={{0,8},{2,10},{4,12},{6,14},{8,16},{10,18},{12,20},{14,22},{16,24},... | collective-permute-start | bytes 1572872 | tf_op jit(solution)/shard_map/ppermute | solution.py:52
  147.3 21.0 %collective-permute-start.13 = (bf16[256,1024]{1,0:T(8,128)(2,1)S(1)}, bf16[256,1024]{1,0:T(8,128)(2,1)S(1)}, u32[]{:S(2)}, u32[]{:S(2)}) collective-permute-start(bf16[256,1024]{1,0:T(8,128)(2,1)S(1)} %collective-permute-done.12), channel_id=1, source_target_pairs={{0,2},{2,0},{4,6},{6,4},{8,10},{10,8},{12,14},{14,12},{16,18},{18,... | collective-permute-start | bytes 1572872 | tf_op jit(solution)/shard_map/ppermute | solution.py:44
  149.5 45.6 %collective-permute-start.29 = (bf16[256,512]{1,0:T(8,128)(2,1)}, bf16[256,512]{1,0:T(8,128)(2,1)S(1)}, u32[]{:S(2)}, u32[]{:S(2)}) collective-permute-start(bf16[256,512]{1,0:T(8,128)(2,1)} %collective-permute-done.27), channel_id=1, source_target_pairs={{0,4},{2,6},{4,0},{6,2},{8,12},{10,14},{12,8},{14,10},{16,20},{18,... | collective-permute-start | bytes 786440 | tf_op jit(solution)/shard_map/ppermute | solution.py:48
  158.5 37.6 %collective-permute-start.22 = (bf16[256,1024]{1,0:T(8,128)(2,1)}, bf16[256,1024]{1,0:T(8,128)(2,1)}, u32[]{:S(2)}, u32[]{:S(2)}) collective-permute-start(bf16[256,1024]{1,0:T(8,128)(2,1)} %pad_maximum_fusion.30), channel_id=1, source_target_pairs={{0,4},{2,6},{4,0},{6,2},{8,12},{10,14},{12,8},{14,10},{16,20},{18,... | collective-permute-start | bytes 1572872 | tf_op jit(solution)/shard_map/ppermute | solution.py:48
  168.2 28.5 %collective-permute-start.21 = (bf16[256,1024]{1,0:T(8,128)(2,1)}, bf16[256,1024]{1,0:T(8,128)(2,1)}, u32[]{:S(2)}, u32[]{:S(2)}) collective-permute-start(bf16[256,1024]{1,0:T(8,128)(2,1)} %pad_maximum_fusion.30), channel_id=1, source_target_pairs={{0,2},{2,0},{4,6},{6,4},{8,10},{10,8},{12,14},{14,12},{16,18},{18,... | collective-permute-start | bytes 1572872 | tf_op jit(solution)/shard_map/ppermute | solution.py:44
  169.0 27.8 %collective-permute-start.18 = (bf16[256,1024]{1,0:T(8,128)(2,1)}, bf16[256,1024]{1,0:T(8,128)(2,1)}, u32[]{:S(2)}, u32[]{:S(2)}) collective-permute-start(bf16[256,1024]{1,0:T(8,128)(2,1)} %pad_maximum_fusion.29), channel_id=1, source_target_pairs={{0,2},{2,0},{4,6},{6,4},{8,10},{10,8},{12,14},{14,12},{16,18},{18,... | collective-permute-start | bytes 1572872 | tf_op jit(solution)/shard_map/ppermute | solution.py:44
  170.6 28.9 %collective-permute-start.36 = (bf16[4,64,1024]{2,1,0:T(8,128)(2,1)}, bf16[4,64,1024]{2,1,0:T(8,128)(2,1)}, u32[]{:S(2)}, u32[]{:S(2)}) collective-permute-start(bf16[4,64,1024]{2,1,0:T(8,128)(2,1)} %collective-permute-done.35), channel_id=1, source_target_pairs={{0,8},{2,10},{4,12},{6,14},{8,16},{10,18},{12,20},{14,22},{16,24},... | collective-permute-start | bytes 1572872 | tf_op jit(solution)/shard_map/ppermute | solution.py:52
  196.7 21.5 %collective-permute-start.14 = (f32[256,1024]{0,1:T(8,128)S(1)}, f32[256,1024]{0,1:T(8,128)S(1)}, u32[]{:S(2)}, u32[]{:S(2)}) collective-permute-start(f32[256,1024]{0,1:T(8,128)S(1)} %fusion.54), channel_id=1, source_target_pairs={{0,1},{1,0},{2,3},{3,2},{4,5},{5,4},{6,7},{7,6},{8,9},{9,8},{10,11... | collective-permute-start | bytes 3145736 | tf_op jit(solution)/shard_map/ppermute | solution.py:60
  196.8 18.9 %collective-permute-start.20 = (bf16[256,1024]{1,0:T(8,128)(2,1)}, bf16[256,1024]{1,0:T(8,128)(2,1)S(1)}, u32[]{:S(2)}, u32[]{:S(2)}) collective-permute-start(bf16[256,1024]{1,0:T(8,128)(2,1)} %collective-permute-done.18), channel_id=1, source_target_pairs={{0,4},{2,6},{4,0},{6,2},{8,12},{10,14},{12,8},{14,10},{16,20},{18,... | collective-permute-start | bytes 1572872 | tf_op jit(solution)/shard_map/ppermute | solution.py:48
  199.4 16.3 %collective-permute-start.37 = (bf16[4,64,1024]{2,1,0:T(8,128)(2,1)}, bf16[4,64,1024]{2,1,0:T(8,128)(2,1)S(1)}, u32[]{:S(2)}, u32[]{:S(2)}) collective-permute-start(bf16[4,64,1024]{2,1,0:T(8,128)(2,1)} %collective-permute-done.36), channel_id=1, source_target_pairs={{0,8},{2,10},{4,12},{6,14},{8,16},{10,18},{12,20},{14,22},{16,24},... | collective-permute-start | bytes 1572872 | tf_op jit(solution)/shard_map/ppermute | solution.py:52
  249.7 25.6 %collective-permute-start.39 = (bf16[256,1024]{0,1:T(8,128)(2,1)S(1)}, bf16[256,1024]{0,1:T(8,128)(2,1)S(1)}, u32[]{:S(2)}, u32[]{:S(2)}) collective-permute-start(bf16[256,1024]{0,1:T(8,128)(2,1)S(1)} %fusion.20), channel_id=1, source_target_pairs={{0,1},{1,0},{2,3},{3,2},{4,5},{5,4},{6,7},{7,6},{8,9},{9,8},{10,11... | collective-permute-start | bytes 1572872 | tf_op jit(solution)/shard_map/ppermute | solution.py:60
  250.8 54.5 %collective-permute-start.59 = (bf16[256,512]{1,0:T(8,128)(2,1)}, bf16[256,512]{1,0:T(8,128)(2,1)}, u32[]{:S(2)}, u32[]{:S(2)}) collective-permute-start(bf16[256,512]{1,0:T(8,128)(2,1)} %get-tuple-element.81), channel_id=1, source_target_pairs={{0,4},{2,6},{4,0},{6,2},{8,12},{10,14},{12,8},{14,10},{16,20},{18,... | collective-permute-start | bytes 786440 | tf_op jit(solution)/shard_map/ppermute | solution.py:48
  256.8 47.9 %collective-permute-start.61 = (bf16[256,512]{1,0:T(8,128)(2,1)}, bf16[256,512]{1,0:T(8,128)(2,1)}, u32[]{:S(2)}, u32[]{:S(2)}) collective-permute-start(bf16[256,512]{1,0:T(8,128)(2,1)} %get-tuple-element.79), channel_id=1, source_target_pairs={{0,2},{2,0},{4,6},{6,4},{8,10},{10,8},{12,14},{14,12},{16,18},{18,... | collective-permute-start | bytes 786440 | tf_op jit(solution)/shard_map/ppermute | solution.py:44
  258.8 55.2 %collective-permute-start.58 = (bf16[256,512]{1,0:T(8,128)(2,1)}, bf16[256,512]{1,0:T(8,128)(2,1)}, u32[]{:S(2)}, u32[]{:S(2)}) collective-permute-start(bf16[256,512]{1,0:T(8,128)(2,1)} %get-tuple-element.82), channel_id=1, source_target_pairs={{0,4},{2,6},{4,0},{6,2},{8,12},{10,14},{12,8},{14,10},{16,20},{18,... | collective-permute-start | bytes 786440 | tf_op jit(solution)/shard_map/ppermute | solution.py:48
  271.0 16.6 %collective-permute-start.67 = (bf16[4,64,1024]{2,1,0:T(8,128)(2,1)}, bf16[4,64,1024]{2,1,0:T(8,128)(2,1)}, u32[]{:S(2)}, u32[]{:S(2)}) collective-permute-start(bf16[4,64,1024]{2,1,0:T(8,128)(2,1)} %fusion.60), channel_id=1, source_target_pairs={{0,24},{2,26},{4,28},{6,30},{8,0},{10,2},{12,4},{14,6},{16,8},{18,... | collective-permute-start | bytes 1572872 | tf_op jit(solution)/shard_map/ppermute | solution.py:56
  275.2 80.1 %collective-permute-start.52 = (bf16[256,1024]{1,0:T(8,128)(2,1)}, bf16[256,1024]{1,0:T(8,128)(2,1)}, u32[]{:S(2)}, u32[]{:S(2)}) collective-permute-start(bf16[256,1024]{1,0:T(8,128)(2,1)} %get-tuple-element.86), channel_id=1, source_target_pairs={{0,2},{2,0},{4,6},{6,4},{8,10},{10,8},{12,14},{14,12},{16,18},{18,... | collective-permute-start | bytes 1572872 | tf_op jit(solution)/shard_map/ppermute | solution.py:44
  304.7 52.3 %collective-permute-start.50 = (bf16[256,1024]{1,0:T(8,128)(2,1)}, bf16[256,1024]{1,0:T(8,128)(2,1)}, u32[]{:S(2)}, u32[]{:S(2)}) collective-permute-start(bf16[256,1024]{1,0:T(8,128)(2,1)} %get-tuple-element.88), channel_id=1, source_target_pairs={{0,4},{2,6},{4,0},{6,2},{8,12},{10,14},{12,8},{14,10},{16,20},{18,... | collective-permute-start | bytes 1572872 | tf_op jit(solution)/shard_map/ppermute | solution.py:48
  305.2 150.3 %collective-permute-start.49 = (bf16[256,1024]{1,0:T(8,128)(2,1)}, bf16[256,1024]{1,0:T(8,128)(2,1)}, u32[]{:S(2)}, u32[]{:S(2)}) collective-permute-start(bf16[256,1024]{1,0:T(8,128)(2,1)} %get-tuple-element.89), channel_id=1, source_target_pairs={{0,4},{2,6},{4,0},{6,2},{8,12},{10,14},{12,8},{14,10},{16,20},{18,... | collective-permute-start | bytes 1572872 | tf_op jit(solution)/shard_map/ppermute | solution.py:48
  325.8 26.8 %collective-permute-start.44 = (bf16[256,1024]{1,0:T(8,128)(2,1)}, bf16[256,1024]{1,0:T(8,128)(2,1)}, u32[]{:S(2)}, u32[]{:S(2)}) collective-permute-start(bf16[256,1024]{1,0:T(8,128)(2,1)} %get-tuple-element.91), channel_id=1, source_target_pairs={{0,2},{2,0},{4,6},{6,4},{8,10},{10,8},{12,14},{14,12},{16,18},{18,... | collective-permute-start | bytes 1572872 | tf_op jit(solution)/shard_map/ppermute | solution.py:44
  328.9 19.7 %collective-permute-start.68 = (bf16[4,64,1024]{2,1,0:T(8,128)(2,1)}, bf16[4,64,1024]{2,1,0:T(8,128)(2,1)}, u32[]{:S(2)}, u32[]{:S(2)}) collective-permute-start(bf16[4,64,1024]{2,1,0:T(8,128)(2,1)} %fusion.39), channel_id=1, source_target_pairs={{0,24},{2,26},{4,28},{6,30},{8,0},{10,2},{12,4},{14,6},{16,8},{18,... | collective-permute-start | bytes 1572872 | tf_op jit(solution)/shard_map/ppermute | solution.py:56
  336.5 45.2 %all-to-all-start.3 = ((bf16[16,2,256]{2,1,0:T(2,128)(2,1)}), bf16[16,2,256]{2,1,0:T(2,128)(2,1)}, u32[]{:S(2)}, u32[]{:S(2)}) async-start(bf16[16,2,256]{2,1,0:T(2,128)(2,1)} %reshape.1028), calls=%async_computation.3 | async-start | bytes 32768 | tf_op jit(solution)/shard_map/all_to_all | solution.py:140
  348.6 15.1 %collective-permute-start.54 = (bf16[256,1024]{1,0:T(8,128)(2,1)}, bf16[256,1024]{1,0:T(8,128)(2,1)S(1)}, u32[]{:S(2)}, u32[]{:S(2)}) collective-permute-start(bf16[256,1024]{1,0:T(8,128)(2,1)} %fusion.43), channel_id=1, source_target_pairs={{0,4},{2,6},{4,0},{6,2},{8,12},{10,14},{12,8},{14,10},{16,20},{18,... | collective-permute-start | bytes 1572872 | tf_op jit(solution)/shard_map/ppermute | solution.py:48
  352.7 22.2 %collective-permute-start.41 = (bf16[256,1024]{1,0:T(8,128)(2,1)S(1)}, bf16[256,1024]{1,0:T(8,128)(2,1)S(1)}, u32[]{:S(2)}, u32[]{:S(2)}) collective-permute-start(bf16[256,1024]{1,0:T(8,128)(2,1)S(1)} %copy-done.70), channel_id=1, source_target_pairs={{0,4},{2,6},{4,0},{6,2},{8,12},{10,14},{12,8},{14,10},{16,20},{18,... | collective-permute-start | bytes 1572872 | tf_op jit(solution)/shard_map/ppermute | solution.py:48
  355.4 84.0 %collective-permute-start.43 = (bf16[256,1024]{1,0:T(8,128)(2,1)}, bf16[256,1024]{1,0:T(8,128)(2,1)}, u32[]{:S(2)}, u32[]{:S(2)}) collective-permute-start(bf16[256,1024]{1,0:T(8,128)(2,1)} %get-tuple-element.90), channel_id=1, source_target_pairs={{0,2},{2,0},{4,6},{6,4},{8,10},{10,8},{12,14},{14,12},{16,18},{18,... | collective-permute-start | bytes 1572872 | tf_op jit(solution)/shard_map/ppermute | solution.py:44
  357.0 86.3 %collective-permute-start.40 = (bf16[256,1024]{1,0:T(8,128)(2,1)}, bf16[256,1024]{1,0:T(8,128)(2,1)}, u32[]{:S(2)}, u32[]{:S(2)}) collective-permute-start(bf16[256,1024]{1,0:T(8,128)(2,1)} %get-tuple-element.94), channel_id=1, source_target_pairs={{0,4},{2,6},{4,0},{6,2},{8,12},{10,14},{12,8},{14,10},{16,20},{18,... | collective-permute-start | bytes 1572872 | tf_op jit(solution)/shard_map/ppermute | solution.py:48
  374.9 66.1 %collective-permute-start.45 = (bf16[256,1024]{1,0:T(8,128)(2,1)}, bf16[256,1024]{1,0:T(8,128)(2,1)}, u32[]{:S(2)}, u32[]{:S(2)}) collective-permute-start(bf16[256,1024]{1,0:T(8,128)(2,1)} %fusion.31), channel_id=1, source_target_pairs={{0,4},{2,6},{4,0},{6,2},{8,12},{10,14},{12,8},{14,10},{16,20},{18,... | collective-permute-start | bytes 1572872 | tf_op jit(solution)/shard_map/ppermute | solution.py:48
  389.6 53.7 %collective-permute-start.42 = (bf16[256,1024]{1,0:T(8,128)(2,1)}, bf16[256,1024]{1,0:T(8,128)(2,1)}, u32[]{:S(2)}, u32[]{:S(2)}) collective-permute-start(bf16[256,1024]{1,0:T(8,128)(2,1)} %fusion.37), channel_id=1, source_target_pairs={{0,2},{2,0},{4,6},{6,4},{8,10},{10,8},{12,14},{14,12},{16,18},{18,... | collective-permute-start | bytes 1572872 | tf_op jit(solution)/shard_map/ppermute | solution.py:44
  444.8 15.7 %collective-permute-start.46 = (bf16[64,2048]{1,0:T(8,128)(2,1)S(1)}, bf16[64,2048]{1,0:T(8,128)(2,1)S(1)}, u32[]{:S(2)}, u32[]{:S(2)}) collective-permute-start(bf16[64,2048]{1,0:T(8,128)(2,1)S(1)} %fusion.82), channel_id=1, source_target_pairs={{0,24},{2,26},{4,28},{6,30},{8,0},{10,2},{12,4},{14,6},{16,8},{18,... | collective-permute-start | bytes 786440 | tf_op jit(solution)/shard_map/ppermute | solution.py:56
  (157 other events, 1705.7 us)
